TPU v7x, 32 devices: a whole 2x2x4 slice. The times are simulated.
32 devices in a mesh: group: 8 (over z, y), inner: 4 (over x, core).
Axes of the slice: x: 2, y: 2, z: 4, core: 2. Of those that a mesh axis runs over, the one named last changes fastest.
Arguments:
- tokens: bfloat16 [12288, 4096], P(('group', 'inner')), may hold values from -6 to 6
- master_weight: float32 [4096, 768], P('inner', 'group'), may hold values from -0.09375 to 0.09375
- first_moment: float32 [4096, 768], P('inner', 'group'), may hold values from -6 to 6
- second_moment: float32 [4096, 768], P('inner', 'group'), may hold values from 0.1 to 10
- gradient: float32 [4096, 768], P('inner', 'group'), may hold values from -6 to 6
- gate_weight: bfloat16 [4096, 2], P('inner'), may hold values from -0.09375 to 0.09375
- input_bias: float32 [1], replicated, may hold values from -3 to -1
- forget_bias: float32 [1], replicated, may hold values from 2 to 5
Outputs:
- new_master: float32 [4096, 768], P('inner', 'group')
- new_first: float32 [4096, 768], P('inner', 'group')
- new_second: float32 [4096, 768], P('inner', 'group')
- hidden: bfloat16 [12288, 256], P(('group', 'inner'))
All inputs are finite; a program needn't handle non-finite values.
Results may differ from a plain program's by a relative error of at most 0.012.
Values may be sent and summed in bfloat16 or wider, within the bound.
No kernel may reach another device: no remote copies, remote signals or barrier semaphores. Data moves between devices by JAX's collectives and lax.ppermute only.
A program may use at most 64 MiB of HBM per device.

v0:
```python
import jax
import jax.numpy as jnp
from jax import lax
from jax.sharding import PartitionSpec as P

QK = 256


beta_first = 0.9
beta_second = 0.999
learn_rate = 0.001
adam_eps = 1e-08
fix_first = 1.0 - (0.9**10) ** 10
fix_second = 1.0 - (0.999**10) ** 10


def mlstm_head(sequence, projected, gate_pre, input_bias, forget_bias):
    query_rows = projected[:, :QK].astype(jnp.bfloat16)
    key_rows = projected[:, QK : 2 * QK].astype(jnp.bfloat16)
    value_rows = projected[:, 2 * QK :].astype(jnp.bfloat16)
    input_gate = gate_pre[:, 0] + input_bias[0]
    forget_log = jax.nn.log_sigmoid(gate_pre[:, 1] + forget_bias[0])
    cumulative = jnp.cumsum(forget_log)
    row_count = sequence.shape[0]
    causal = jnp.arange(row_count)[:, None] >= jnp.arange(row_count)[None, :]
    decay_log = cumulative[:, None] - cumulative[None, :] + input_gate[None, :]
    decay_matrix = jnp.exp(jnp.where(causal, decay_log, -jnp.inf))
    scores = jnp.dot(query_rows, key_rows.T, preferred_element_type=jnp.float32) * QK ** (-0.5)
    weighted = scores * decay_matrix
    normalizer = jnp.sum(weighted, axis=1)
    numerator = jnp.dot(
        weighted.astype(jnp.bfloat16), value_rows, preferred_element_type=jnp.float32
    )
    return (numerator / jnp.maximum(jnp.abs(normalizer), 1.0)[:, None]).astype(jnp.bfloat16)


def on_device(
    tokens,
    master_weight,
    first_moment,
    second_moment,
    gradient,
    gate_weight,
    input_bias,
    forget_bias,
):
    new_first = beta_first * first_moment + (1.0 - beta_first) * gradient
    new_second = beta_second * second_moment + (1.0 - beta_second) * gradient * gradient
    new_master = master_weight - learn_rate * (new_first / fix_first) / (
        jnp.sqrt(new_second / fix_second) + adam_eps
    )
    sendable = new_master.astype(jnp.bfloat16)
    secondary = lax.all_gather(sendable, "group", axis=1, tiled=True)
    projected = jnp.dot(
        tokens,
        lax.all_gather(secondary, "inner", axis=0, tiled=True),
        preferred_element_type=jnp.float32,
    )
    gate_pre = jnp.dot(
        tokens,
        lax.all_gather(gate_weight, "inner", axis=0, tiled=True),
        preferred_element_type=jnp.float32,
    )
    hidden = mlstm_head(tokens, projected, gate_pre, input_bias, forget_bias)
    return (new_master, new_first, new_second, hidden)


def solution(mesh):
    placed = (
        P(("group", "inner"), None),
        P("inner", "group"),
        P("inner", "group"),
        P("inner", "group"),
        P("inner", "group"),
        P("inner", None),
        P(),
        P(),
    )
    return jax.shard_map(
        on_device,
        mesh=mesh,
        in_specs=placed,
        out_specs=(
            P("inner", "group"),
            P("inner", "group"),
            P("inner", "group"),
            P(("group", "inner"), None),
        ),
        check_vma=False,
    )
```

profile of v0, /device:TPU:0, one launch (start us, length us, event | category | flops | bytes accessed | tf_op | source)
XLA Modules:
  0.0 118.3 jit_solution(17927915821173134187)
XLA Ops:
  7.2 0.0 copy-start
  7.2 0.0 copy-start.1
  7.2 0.0 all-gather.3.cloned.1.call-start
  7.2 2.7 %fusion.16 = (bf16[1024,96]{0,1:T(8,128)(2,1)}, f32[1024,96]{0,1:T(8,128)}, f32[1024,96]{0,1:T(8,128)}, f32[1024,96]{0,1:T(8,128)}) fusion(f32[1024,96]{0,1:T(8,128)} %param.9, f32[1024,96]{0,1:T(8,128)} %param.12, f32[1024,96]{0,1:T(8,128)} %param.10, f32[1024,96]{0,1:T(8,128)} %param.11), kind=kLoop, calls=%fused_computation.31 | loop fusion | flops 1277952 | bytes 2949120 | tf_op jit(solution)/shard_map/convert_element_type | solution.py:52
  10.0 0.0 all-gather.3.cloned.1.call-update
  10.0 0.0 all-gather.5.cloned.1.call-start
  10.0 47.7 %all-gather.3.cloned.1.call-done = bf16[1024,768]{0,1:T(8,128)(2,1)} async-done(((bf16[1024,96]{0,1:T(8,128)(2,1)}), bf16[1024,768]{0,1:T(8,128)(2,1)}) %all-gather.3.cloned.1.call-update) | async-done | bytes 1572880 | tf_op jit(solution)/shard_map/all_gather | solution.py:53
  57.7 0.0 all-gather.5.cloned.1.call-update
  59.0 0.0 copy-done.1
  59.0 5.2 %all_gather.11 = bf16[4096,2]{0,1:T(2,128)(2,1)S(1)} all-gather(bf16[1024,2]{0,1:T(2,128)(2,1)S(1)} %copy-done.1), channel_id=1, replica_groups=mesh['group'=8,'inner'=4] {'inner'}, dimensions={0}, use_global_device_ids=true | all-gather | bytes 20480 | tf_op jit(solution)/shard_map/all_gather | solution.py:61
  64.2 0.0 copy-done
  64.2 0.9 fusion.19
  65.2 0.3 reduce-window.9
  65.5 0.1 slice.28
  65.6 0.1 slice_reduce_fusion
  65.7 0.1 add_bitcast_fusion
  65.8 38.7 %all-gather.5.cloned.1.call-done = bf16[4096,768]{0,1:T(8,128)(2,1)} async-done(((bf16[1024,768]{0,1:T(8,128)(2,1)}), bf16[4096,768]{0,1:T(8,128)(2,1)}) %all-gather.5.cloned.1.call-update) | async-done | bytes 6291472 | tf_op jit(solution)/shard_map/all_gather | solution.py:56
  104.5 5.6 %fusion = bf16[384,768]{0,1:T(8,128)(2,1)S(1)} fusion(bf16[4096,768]{0,1:T(8,128)(2,1)} %all-gather.5.cloned.1.call-done, bf16[384,4096]{1,0:T(8,128)(2,1)S(1)} %copy-done), kind=kOutput, calls=%fused_computation.1 | convolution fusion | flops 2416214016 | bytes 10027008 | tf_op jit(solution)/shard_map/dot_general | solution.py:54
  110.1 0.3 fusion.18
  110.4 1.0 fusion.2
  (4 shorter events, 0.1 us)
Async XLA Ops:
  7.2 57.1 %copy-start = (bf16[384,4096]{1,0:T(8,128)(2,1)S(1)}, bf16[384,4096]{1,0:T(8,128)(2,1)}, u32[]{:S(2)}) copy-start(bf16[384,4096]{1,0:T(8,128)(2,1)} %param.8) | copy-start | bytes 9437188
  7.2 51.8 %copy-start.1 = (bf16[1024,2]{0,1:T(2,128)(2,1)S(1)}, bf16[1024,2]{0,1:T(2,128)(2,1)}, u32[]{:S(2)}) copy-start(bf16[1024,2]{0,1:T(2,128)(2,1)} %param.13) | copy-start | bytes 12292
  7.2 50.5 %all-gather.3.cloned.1.call-start = ((), (), s32[]{:S(2)}) async-start(), calls=%async_computation | async-start | bytes 1769472 | tf_op jit(solution)/shard_map/all_gather | solution.py:53
  10.0 94.5 %all-gather.5.cloned.1.call-start = ((), (), s32[]{:S(2)}) async-start(), calls=%async_computation.1 | async-start | bytes 7864320 | tf_op jit(solution)/shard_map/all_gather | solution.py:56
Sparse Core Ops, SparseCore 0:
  10.8 46.8 all-gather.2
  59.3 45.1 all-gather.4
where the time goes:
time: 118 us
  waiting for transfers between devices  86.4 us (73%)
  between operations  15.4 us (13%)
  matrix products  7.83 us (7%)
  blocking collectives  5.19 us (4%)
  other arithmetic  3.21 us (3%)
    all_gather x1, waiting for transfers between devices, on_device(): secondary = lax.all_gather(sendable, 'group', axis=1, tiled=True)  47.7 us
    all_gather x1, waiting for transfers between devices, on_device(): lax.all_gather(secondary, 'inner', axis=0, tiled=True)  38.7 us
    dot_general x1, matrix products, on_device(): jnp.dot(tokens, lax.all_gather(secondary, 'inner', axis=0, tiled=True), p...  5.59 us
    all_gather x1, blocking collectives, on_device(): lax.all_gather(gate_weight, 'inner', axis=0, tiled=True)  5.19 us
    convert_element_type x1, other arithmetic, on_device(): sendable = new_master.astype(jnp.bfloat16)  2.73 us
  transfers between devices with their start and end apart: 2, of which 2 were waited for; matrix products, arithmetic and copies ran while one was open for 1% of the time, Pallas kernels for 0%

commit v1 on v0

--- a/solution.py
+++ b/solution.py
@@ -1,6 +1,11 @@
+import functools
+import itertools
+
 import jax
 import jax.numpy as jnp
 from jax import lax
+from jax.experimental import pallas as pl
+from jax.experimental.pallas import tpu as pltpu
 from jax.sharding import PartitionSpec as P
 
 QK = 256
@@ -12,6 +17,19 @@
 adam_eps = 1e-08
 fix_first = 1.0 - (0.9**10) ** 10
 fix_second = 1.0 - (0.999**10) ** 10
+
+AXES = ("group", "inner")
+NT = (((1,), (1,)), ((), ()))
+TN = (((0,), (0,)), ((), ()))
+
+
+def adam(first_moment, second_moment, master_weight, gradient):
+    new_first = beta_first * first_moment + (1.0 - beta_first) * gradient
+    new_second = beta_second * second_moment + (1.0 - beta_second) * gradient * gradient
+    new_master = master_weight - learn_rate * (new_first / fix_first) / (
+        jnp.sqrt(new_second / fix_second) + adam_eps
+    )
+    return new_master, new_first, new_second
 
 
 def mlstm_head(sequence, projected, gate_pre, input_bias, forget_bias):
@@ -34,21 +52,10 @@
     return (numerator / jnp.maximum(jnp.abs(normalizer), 1.0)[:, None]).astype(jnp.bfloat16)
 
 
-def on_device(
-    tokens,
-    master_weight,
-    first_moment,
-    second_moment,
-    gradient,
-    gate_weight,
-    input_bias,
-    forget_bias,
+def gathered_everywhere(
+    tokens, master_weight, first_moment, second_moment, gradient, gate_weight, input_bias, forget_bias
 ):
-    new_first = beta_first * first_moment + (1.0 - beta_first) * gradient
-    new_second = beta_second * second_moment + (1.0 - beta_second) * gradient * gradient
-    new_master = master_weight - learn_rate * (new_first / fix_first) / (
-        jnp.sqrt(new_second / fix_second) + adam_eps
-    )
+    new_master, new_first, new_second = adam(first_moment, second_moment, master_weight, gradient)
     sendable = new_master.astype(jnp.bfloat16)
     secondary = lax.all_gather(sendable, "group", axis=1, tiled=True)
     projected = jnp.dot(
@@ -63,6 +70,218 @@
     )
     hidden = mlstm_head(tokens, projected, gate_pre, input_bias, forget_bias)
     return (new_master, new_first, new_second, hidden)
+
+
+NZ, NY, NX, NC = 4, 2, 2, 2
+
+
+def permutation(target):
+    pairs = []
+    for z, y, x, c in itertools.product(range(NZ), range(NY), range(NX), range(NC)):
+        to_z, to_y, to_x, to_c = target(z, y, x, c)
+        pairs.append((((z * NY + y) * NX + x) * NC + c, ((to_z * NY + to_y) * NX + to_x) * NC + to_c))
+    return pairs
+
+
+OTHER_CORE = permutation(lambda z, y, x, c: (z, y, x, 1 - c))
+OTHER_X = permutation(lambda z, y, x, c: (z, y, 1 - x, c))
+NEXT_Z = permutation(lambda z, y, x, c: ((z + 1) % NZ, y, x, c))
+FIRST = permutation(lambda z, y, x, c: (z, y, 1 - x, c) if c == 0 else (z, 1 - y, x, c))
+SECOND = permutation(lambda z, y, x, c: (z, 1 - y, x, c) if c == 0 else (z, y, 1 - x, c))
+
+
+def send(block, pairs):
+    return lax.ppermute(block, AXES, pairs)
+
+
+def place():
+    group, inner = lax.axis_index("group"), lax.axis_index("inner")
+    return group // NY, group % NY, inner // NC, inner % NC
+
+
+def adam_kernel(master_ref, first_ref, second_ref, grad_ref, to_master, to_first, to_second, to_send):
+    new_master, new_first, new_second = adam(
+        first_ref[...], second_ref[...], master_ref[...], grad_ref[...]
+    )
+    to_master[...] = new_master
+    to_first[...] = new_first
+    to_second[...] = new_second
+    to_send[...] = new_master.astype(jnp.bfloat16)
+
+
+def adam_step(master, first, second, grad):
+    columns, rows = master.shape
+    steps = 3
+    spec = pl.BlockSpec((columns // steps, rows), lambda i: (i, 0))
+    wide = jax.ShapeDtypeStruct(master.shape, jnp.float32)
+    return pl.pallas_call(
+        adam_kernel,
+        grid=(steps,),
+        in_specs=[spec] * 4,
+        out_specs=[spec] * 4,
+        out_shape=[wide, wide, wide, jax.ShapeDtypeStruct(master.shape, jnp.bfloat16)],
+        name="adam",
+    )(master, first, second, grad)
+
+
+def project_kernel(with_gate, own_block, first_block, second_block, third_block, *rest):
+    if with_gate:
+        own_gate, other_gate, tokens, tokens_other, out_own, out_send, stack, held, piece_sem, token_sem = rest
+    else:
+        tokens, tokens_other, out_own, out_send, stack, held, piece_sem, token_sem = rest
+    _, y, x, c = place()
+    columns, depth = own_block.shape
+    here = pl.multiple_of(y * columns, 16)
+    there = pl.multiple_of((1 - y) * columns, 16)
+    swap = c == 0
+    spots = [
+        (own_block, 0, here),
+        (first_block, jnp.where(swap, 1, 0), jnp.where(swap, here, there)),
+        (second_block, jnp.where(swap, 0, 1), jnp.where(swap, there, here)),
+        (third_block, 1, there),
+    ]
+    copies = []
+    for side, its_x in enumerate((x, 1 - x)):
+        at = pl.multiple_of((its_x * NC + c) * depth, depth)
+        for which, source in enumerate((tokens, tokens_other)):
+            copies.append(
+                pltpu.make_async_copy(
+                    source.at[:, pl.ds(at, depth)], held.at[side, which], token_sem.at[side, which]
+                )
+            )
+    pieces = [
+        pltpu.make_async_copy(
+            source, stack.at[side, pl.ds(pl.multiple_of(row, 16), columns)], piece_sem.at[n]
+        )
+        for n, (source, side, row) in enumerate(spots)
+    ]
+    for copy in pieces + copies:
+        copy.start()
+    if with_gate:
+        for side, gate in enumerate((own_gate, other_gate)):
+            stack[side, NY * columns :] = jnp.concatenate(
+                [gate[...], jnp.zeros((16 - gate.shape[0], depth), jnp.bfloat16)], axis=0
+            )
+    for copy in pieces:
+        copy.wait()
+    sums = [None, None]
+    for side in range(2):
+        for which in range(2):
+            copies[side * 2 + which].wait()
+            part = lax.dot_general(
+                stack[side], held[side, which], NT, preferred_element_type=jnp.float32
+            )
+            sums[which] = part if side == 0 else sums[which] + part
+    out_own[...] = sums[0]
+    out_send[...] = sums[1]
+
+
+def project(blocks, gates, tokens, tokens_other):
+    columns, depth = blocks[0].shape
+    rows = NY * columns + (16 if gates else 0)
+    sequence = tokens.shape[0]
+    any_spec = pl.BlockSpec(memory_space=pl.ANY)
+    vmem_spec = pl.BlockSpec(memory_space=pltpu.VMEM)
+    out = jax.ShapeDtypeStruct((rows, sequence), jnp.float32)
+    return pl.pallas_call(
+        functools.partial(project_kernel, bool(gates)),
+        in_specs=[any_spec] * 4 + [vmem_spec] * len(gates) + [any_spec] * 2,
+        out_specs=[vmem_spec] * 2,
+        out_shape=[out, out],
+        scratch_shapes=[
+            pltpu.VMEM((2, rows, depth), jnp.bfloat16),
+            pltpu.VMEM((2, 2, sequence, depth), jnp.bfloat16),
+            pltpu.SemaphoreType.DMA((4,)),
+            pltpu.SemaphoreType.DMA((2, 2)),
+        ],
+        compiler_params=pltpu.CompilerParams(vmem_limit_bytes=20 * 2**20),
+        cost_estimate=pl.CostEstimate(
+            flops=2 * 2 * 2 * rows * depth * sequence, bytes_accessed=2 * 4 * sequence * depth, transcendentals=0
+        ),
+        name="project",
+    )(*blocks, *gates, tokens, tokens_other)
+
+
+def head_kernel(own_0, own_1, own_2, own_3, got_0, got_1, got_2, got_3, input_bias, forget_bias, out, projected):
+    z, _, _, _ = place()
+    columns = own_1.shape[0]
+    sequence = own_1.shape[1]
+    for offset, (own, got) in enumerate(((own_0, got_0), (own_1, got_1), (own_2, got_2), (own_3, got_3))):
+        at = pl.multiple_of(lax.rem(z + NZ - offset, NZ) * columns, 16)
+        projected[pl.ds(at, columns)] = (own[:columns] + got[:columns]).astype(jnp.bfloat16)
+    gate_pre = own_0[columns : columns + 8] + got_0[columns : columns + 8]
+    input_gate = gate_pre[0:1] + input_bias[0]
+    cumulative = jax.nn.log_sigmoid(gate_pre[1:2] + forget_bias[0])
+    lane = lax.broadcasted_iota(jnp.int32, (1, sequence), 1)
+    step = 1
+    while step < sequence:
+        cumulative = cumulative + jnp.where(lane >= step, pltpu.roll(cumulative, step, 1), 0.0)
+        step *= 2
+    source = jnp.broadcast_to(input_gate - cumulative, (8, sequence)).T[:, 0:1]
+    to_t = lax.broadcasted_iota(jnp.int32, (sequence, sequence), 1)
+    from_s = lax.broadcasted_iota(jnp.int32, (sequence, sequence), 0)
+    decay = jnp.exp(jnp.where(from_s <= to_t, cumulative + source, -jnp.inf))
+    query, key, value = (projected[n * QK : (n + 1) * QK] for n in range(3))
+    scores = lax.dot_general(key, query, TN, preferred_element_type=jnp.float32) * QK ** (-0.5)
+    weighted = scores * decay
+    normalizer = jnp.sum(weighted, axis=0, keepdims=True)
+    numerator = jnp.dot(value, weighted.astype(jnp.bfloat16), preferred_element_type=jnp.float32)
+    out[...] = (numerator / jnp.maximum(jnp.abs(normalizer), 1.0)).T.astype(jnp.bfloat16)
+
+
+def head(own, got, input_bias, forget_bias):
+    columns, sequence = own[1].shape
+    vmem_spec = pl.BlockSpec(memory_space=pltpu.VMEM)
+    smem_spec = pl.BlockSpec(memory_space=pltpu.SMEM)
+    return pl.pallas_call(
+        head_kernel,
+        in_specs=[vmem_spec] * 8 + [smem_spec] * 2,
+        out_specs=vmem_spec,
+        out_shape=jax.ShapeDtypeStruct((sequence, NZ * columns - 2 * QK), jnp.bfloat16),
+        scratch_shapes=[pltpu.VMEM((NZ * columns, sequence), jnp.bfloat16)],
+        compiler_params=pltpu.CompilerParams(vmem_limit_bytes=20 * 2**20),
+        name="head",
+    )(*own, *got, input_bias, forget_bias)
+
+
+def after(value, *others):
+    return lax.optimization_barrier((value,) + others)[0]
+
+
+def by_links(
+    tokens, master_weight, first_moment, second_moment, gradient, gate_weight, input_bias, forget_bias
+):
+    new_master, new_first, new_second, block = adam_step(
+        master_weight.T, first_moment.T, second_moment.T, gradient.T
+    )
+    gate = gate_weight.T
+    z1 = send(block, NEXT_Z)
+    a1 = send(block, FIRST)
+    a2 = send(block, SECOND)
+    tokens_other = send(tokens, OTHER_CORE)
+    gate_other = send(gate, OTHER_X)
+    go = after(z1, a1, a2)
+    b1 = send(go, FIRST)
+    a3 = send(a1, SECOND)
+    z2 = send(go, NEXT_Z)
+    b2 = send(go, SECOND)
+    own_a, part_a = project((block, a1, a2, a3), (gate, gate_other), tokens, tokens_other)
+    go = after(z2, b1, a3)
+    c1 = send(go, FIRST)
+    b3 = send(b1, SECOND)
+    z3 = send(go, NEXT_Z)
+    c2 = send(go, SECOND)
+    own_b, part_b = project((z1, b1, b2, b3), (), tokens, tokens_other)
+    go = after(z3, c1, b3)
+    d1 = send(go, FIRST)
+    c3 = send(c1, SECOND)
+    d2 = send(go, SECOND)
+    own_c, part_c = project((z2, c1, c2, c3), (), tokens, tokens_other)
+    d3 = send(d1, SECOND)
+    own_d, part_d = project((z3, d1, d2, d3), (), tokens, tokens_other)
+    got = [send(part, OTHER_CORE) for part in (part_a, part_b, part_c, part_d)]
+    hidden = head((own_a, own_b, own_c, own_d), got, input_bias, forget_bias)
+    return (new_master.T, new_first.T, new_second.T, hidden)
 
 
 def solution(mesh):
@@ -76,8 +295,9 @@
         P(),
         P(),
     )
+    fits = mesh.shape["group"] == NZ * NY and mesh.shape["inner"] == NX * NC
     return jax.shard_map(
-        on_device,
+        by_links if fits else gathered_everywhere,
         mesh=mesh,
         in_specs=placed,
         out_specs=(

time: 118 us -> 67 us (0.57)
  waiting for transfers between devices: 86.4 us -> 25.9 us
  starting transfers between devices: 0.08 us -> 18.1 us
  Pallas kernels: 0 us -> 17.2 us
  between operations: 15.4 us -> 2.05 us
  matrix products: 7.83 us -> 0 us
  blocking collectives: 5.19 us -> 0 us
  local copies, waits for them, and re-layouts: 0.21 us -> 3.51 us
  other arithmetic: 3.21 us -> 0 us
    all_gather x2 -> x0, waiting for transfers between devices: 86.3 us -> none  [the longest x1 47.7 us: on_device(): secondary = lax.all_gather(sendable, 'group', axis=1, tiled=True)]
    ppermute x0 -> x21, waiting for transfers between devices: none -> 25.9 us  [send(): return lax.ppermute(block, AXES, pairs)]
    ppermute x0 -> x21, starting transfers between devices: none -> 18.1 us  [send(): return lax.ppermute(block, AXES, pairs)]
    pallas_call x0 -> x6, Pallas kernels: none -> 17.2 us  [the longest x4 11.9 us: project(): pl.pallas_call(functools.partial(project_kernel, bool(gates)), in_specs=[...]
    dot_general x4 -> x0, matrix products: 7.83 us -> none  [the longest x1 5.59 us: on_device(): jnp.dot(tokens, lax.all_gather(secondary, 'inner', axis=0, tiled=True), p...]
    all_gather x1 -> x0, blocking collectives: 5.19 us -> none  [on_device(): lax.all_gather(gate_weight, 'inner', axis=0, tiled=True)]
    unnamed x4 -> x8, local copies, waits for them, and re-layouts: 0.01 us -> 3.51 us
    convert_element_type x1 -> x0, other arithmetic: 2.73 us -> none  [on_device(): sendable = new_master.astype(jnp.bfloat16)]
  transfers between devices with their start and end apart: 2 -> 21, of which waited for: 2 -> 9; matrix products, arithmetic and copies ran while one was open for 1% -> 0% of each run, Pallas kernels for 0% -> 23%
where the time goes in v1:
time: 67 us; the launch traced here: 66.7 us
  waiting for transfers between devices  25.9 us (39%)
  starting transfers between devices  18.1 us (27%)
  Pallas kernels  17.2 us (26%)
  local copies, waits for them, and re-layouts  3.51 us (5%)
  between operations  2.05 us (3%)
    ppermute x21, waiting for transfers between devices, send(): return lax.ppermute(block, AXES, pairs)  25.9 us
    ppermute x21, starting transfers between devices, send(): return lax.ppermute(block, AXES, pairs)  18.1 us
    pallas_call x4, Pallas kernels, project(): pl.pallas_call(functools.partial(project_kernel, bool(gates)), in_specs=[...  11.9 us
    unnamed x8, local copies, waits for them, and re-layouts  3.51 us
    pallas_call x1, Pallas kernels, adam_step(): pl.pallas_call(adam_kernel, grid=(steps,), in_specs=[spec] * 4, out_specs...  3.4 us
    pallas_call x1, Pallas kernels, head(): pl.pallas_call(head_kernel, in_specs=[vmem_spec] * 8 + [smem_spec] * 2, o...  1.88 us
  transfers between devices with their start and end apart: 21, of which 9 were waited for; matrix products, arithmetic and copies ran while one was open for 0% of the time, Pallas kernels for 23%

profile of v1, /device:TPU:0, one launch (start us, length us, event | category | flops | bytes accessed | tf_op | source)
XLA Modules:
  0.0 66.7 jit_solution(16360512278089047104)
XLA Ops:
  1.1 3.4 %adam.1 = (f32[96,1024]{1,0:T(8,128)}, f32[96,1024]{1,0:T(8,128)}, f32[96,1024]{1,0:T(8,128)}, bf16[96,1024]{1,0:T(8,128)(2,1)}) custom-call(f32[96,1024]{1,0:T(8,128)} %bitcast.10, f32[96,1024]{1,0:T(8,128)} %bitcast.11, f32[96,1024]{1,0:T(8,128)} %bitcast.12, f32[96,1024]{1,0:T(8,128)} %bitcast.13), custom_call_target="tpu_custom_call" | custom-call | tf_op jit(solution)/shard_map/adam/pallas_call | solution.py:117
  4.5 2.6 %collective-permute-start = (bf16[96,1024]{1,0:T(8,128)(2,1)}, bf16[96,1024]{1,0:T(8,128)(2,1)S(1)}, u32[]{:S(2)}, u32[]{:S(2)}) collective-permute-start(bf16[96,1024]{1,0:T(8,128)(2,1)} %get-tuple-element.22.own_block), channel_id=1, source_target_pairs={{0,2},{1,5},{2,0},{3,7},{4,6},{5,1},{6,4},{7,3},{8,10},{9,13},{10,... | collective-permute-start | bytes 589832 | tf_op jit(solution)/shard_map/ppermute | solution.py:94
  7.1 1.5 %collective-permute-start.1 = (bf16[96,1024]{1,0:T(8,128)(2,1)}, bf16[96,1024]{1,0:T(8,128)(2,1)S(1)}, u32[]{:S(2)}, u32[]{:S(2)}) collective-permute-start(bf16[96,1024]{1,0:T(8,128)(2,1)} %get-tuple-element.22.own_block), channel_id=1, source_target_pairs={{0,4},{1,3},{2,6},{3,1},{4,0},{5,7},{6,2},{7,5},{8,12},{9,11},{10,... | collective-permute-start | bytes 589832 | tf_op jit(solution)/shard_map/ppermute | solution.py:94
  8.6 1.6 %collective-permute-start.5 = (bf16[96,1024]{1,0:T(8,128)(2,1)}, bf16[96,1024]{1,0:T(8,128)(2,1)S(1)}, u32[]{:S(2)}, u32[]{:S(2)}) collective-permute-start(bf16[96,1024]{1,0:T(8,128)(2,1)} %get-tuple-element.22.own_block), channel_id=1, source_target_pairs={{0,8},{1,9},{2,10},{3,11},{4,12},{5,13},{6,14},{7,15},{8,16},{9,17... | collective-permute-start | bytes 589832 | tf_op jit(solution)/shard_map/ppermute | solution.py:94
  10.2 1.8 %collective-permute-done.first_block = bf16[96,1024]{1,0:T(8,128)(2,1)S(1)} collective-permute-done((bf16[96,1024]{1,0:T(8,128)(2,1)}, bf16[96,1024]{1,0:T(8,128)(2,1)S(1)}, u32[]{:S(2)}, u32[]{:S(2)}) %collective-permute-start) | collective-permute-done | bytes 196640 | tf_op jit(solution)/shard_map/ppermute | solution.py:94
  12.0 1.0 %collective-permute-done.1.second_block = bf16[96,1024]{1,0:T(8,128)(2,1)S(1)} collective-permute-done((bf16[96,1024]{1,0:T(8,128)(2,1)}, bf16[96,1024]{1,0:T(8,128)(2,1)S(1)}, u32[]{:S(2)}, u32[]{:S(2)}) %collective-permute-start.1) | collective-permute-done | bytes 196640 | tf_op jit(solution)/shard_map/ppermute | solution.py:94
  13.0 4.5 %collective-permute-done.5.own_block = bf16[96,1024]{1,0:T(8,128)(2,1)S(1)} collective-permute-done((bf16[96,1024]{1,0:T(8,128)(2,1)}, bf16[96,1024]{1,0:T(8,128)(2,1)S(1)}, u32[]{:S(2)}, u32[]{:S(2)}) %collective-permute-start.5) | collective-permute-done | bytes 196640 | tf_op jit(solution)/shard_map/ppermute | solution.py:94
  18.5 5.2 %collective-permute-done.2.third_block = bf16[96,1024]{1,0:T(8,128)(2,1)S(1)} collective-permute-done((bf16[96,1024]{1,0:T(8,128)(2,1)S(1)}, bf16[96,1024]{1,0:T(8,128)(2,1)S(1)}, u32[]{:S(2)}, u32[]{:S(2)}) %collective-permute-start.2) | collective-permute-done | bytes 196640 | tf_op jit(solution)/shard_map/ppermute | solution.py:94
  23.7 2.3 %collective-permute-done.9.own_block = bf16[96,1024]{1,0:T(8,128)(2,1)S(1)} collective-permute-done((bf16[96,1024]{1,0:T(8,128)(2,1)S(1)}, bf16[96,1024]{1,0:T(8,128)(2,1)S(1)}, u32[]{:S(2)}, u32[]{:S(2)}) %collective-permute-start.9) | collective-permute-done | bytes 196640 | tf_op jit(solution)/shard_map/ppermute | solution.py:94
  26.0 1.5 %collective-permute-start.8 = (bf16[96,1024]{1,0:T(8,128)(2,1)S(1)}, bf16[96,1024]{1,0:T(8,128)(2,1)S(1)}, u32[]{:S(2)}, u32[]{:S(2)}) collective-permute-start(bf16[96,1024]{1,0:T(8,128)(2,1)S(1)} %collective-permute-done.6.first_block), channel_id=1, source_target_pairs={{0,4},{1,3},{2,6},{3,1},{4,0},{5,7},{6,2},{7,5},{8,12},{9,11},{10,... | collective-permute-start | bytes 589832 | tf_op jit(solution)/shard_map/ppermute | solution.py:94
  27.5 1.5 %collective-permute-start.10 = (bf16[96,1024]{1,0:T(8,128)(2,1)S(1)}, bf16[96,1024]{1,0:T(8,128)(2,1)S(1)}, u32[]{:S(2)}, u32[]{:S(2)}) collective-permute-start(bf16[96,1024]{1,0:T(8,128)(2,1)S(1)} %collective-permute-done.9.own_block), channel_id=1, source_target_pairs={{0,2},{1,5},{2,0},{3,7},{4,6},{5,1},{6,4},{7,3},{8,10},{9,13},{10,... | collective-permute-start | bytes 589832 | tf_op jit(solution)/shard_map/ppermute | solution.py:94
  29.0 2.7 %collective-permute-done.8.third_block = bf16[96,1024]{1,0:T(8,128)(2,1)S(1)} collective-permute-done((bf16[96,1024]{1,0:T(8,128)(2,1)S(1)}, bf16[96,1024]{1,0:T(8,128)(2,1)S(1)}, u32[]{:S(2)}, u32[]{:S(2)}) %collective-permute-start.8) | collective-permute-done | bytes 196640 | tf_op jit(solution)/shard_map/ppermute | solution.py:94
  31.7 1.5 %collective-permute-done.10.first_block = bf16[96,1024]{1,0:T(8,128)(2,1)S(1)} collective-permute-done((bf16[96,1024]{1,0:T(8,128)(2,1)S(1)}, bf16[96,1024]{1,0:T(8,128)(2,1)S(1)}, u32[]{:S(2)}, u32[]{:S(2)}) %collective-permute-start.10) | collective-permute-done | bytes 196640 | tf_op jit(solution)/shard_map/ppermute | solution.py:94
  33.2 3.3 %collective-permute-done.13.own_block = bf16[96,1024]{1,0:T(8,128)(2,1)S(1)} collective-permute-done((bf16[96,1024]{1,0:T(8,128)(2,1)S(1)}, bf16[96,1024]{1,0:T(8,128)(2,1)S(1)}, u32[]{:S(2)}, u32[]{:S(2)}) %collective-permute-start.13) | collective-permute-done | bytes 196640 | tf_op jit(solution)/shard_map/ppermute | solution.py:94
  37.5 1.5 %collective-permute-start.3 = (bf16[2,1024]{1,0:T(2,128)(2,1)}, bf16[2,1024]{1,0:T(2,128)(2,1)S(1)}, u32[]{:S(2)}, u32[]{:S(2)}) collective-permute-start(bf16[2,1024]{1,0:T(2,128)(2,1)} %bitcast.8), channel_id=1, source_target_pairs={{0,2},{1,3},{2,0},{3,1},{4,6},{5,7},{6,4},{7,5},{8,10},{9,11},{10,... | collective-permute-start | bytes 12296 | tf_op jit(solution)/shard_map/ppermute | solution.py:94
  39.0 1.5 %collective-permute-start.11 = (bf16[96,1024]{1,0:T(8,128)(2,1)S(1)}, bf16[96,1024]{1,0:T(8,128)(2,1)S(1)}, u32[]{:S(2)}, u32[]{:S(2)}) collective-permute-start(bf16[96,1024]{1,0:T(8,128)(2,1)S(1)} %collective-permute-done.9.own_block), channel_id=1, source_target_pairs={{0,4},{1,3},{2,6},{3,1},{4,0},{5,7},{6,2},{7,5},{8,12},{9,11},{10,... | collective-permute-start | bytes 589832 | tf_op jit(solution)/shard_map/ppermute | solution.py:94
  40.5 3.7 %collective-permute-done.3.rest_1_ = bf16[2,1024]{1,0:T(2,128)(2,1)S(1)} collective-permute-done((bf16[2,1024]{1,0:T(2,128)(2,1)}, bf16[2,1024]{1,0:T(2,128)(2,1)S(1)}, u32[]{:S(2)}, u32[]{:S(2)}) %collective-permute-start.3) | collective-permute-done | bytes 4128 | tf_op jit(solution)/shard_map/ppermute | solution.py:94
  44.8 1.5 %collective-permute-start.15 = (bf16[96,1024]{1,0:T(8,128)(2,1)S(1)}, bf16[96,1024]{1,0:T(8,128)(2,1)S(1)}, u32[]{:S(2)}, u32[]{:S(2)}) collective-permute-start(bf16[96,1024]{1,0:T(8,128)(2,1)S(1)} %collective-permute-done.13.own_block), channel_id=1, source_target_pairs={{0,4},{1,3},{2,6},{3,1},{4,0},{5,7},{6,2},{7,5},{8,12},{9,11},{10,... | collective-permute-start | bytes 589832 | tf_op jit(solution)/shard_map/ppermute | solution.py:94
  46.8 1.9 %copy-done = bf16[384,4096]{1,0:T(8,128)(2,1)S(1)} copy-done((bf16[384,4096]{1,0:T(8,128)(2,1)S(1)}, bf16[384,4096]{1,0:T(8,128)(2,1)}, u32[]{:S(2)}) %copy-start) | copy-done | bytes 3145752
  50.3 3.0 %project.4 = (f32[208,384]{1,0:T(8,128)S(1)}, f32[208,384]{1,0:T(8,128)S(1)}) custom-call(bf16[96,1024]{1,0:T(8,128)(2,1)S(1)} %copy-done.2, bf16[96,1024]{1,0:T(8,128)(2,1)S(1)} %collective-permute-done.first_block, bf16[96,1024]{1,0:T(8,128)(2,1)S(1)} %collective-permute-done.1.second_block, bf16[96,1024]{1,0:T(8,128)(2,1)S(1)} %collective-permute-done.2.third_block, ...), custom_call_target="tpu_custom_call" | custom-call | flops 654311424 | bytes 3145728 | tf_op jit(solution)/shard_map/project/pallas_call | solution.py:186
  53.4 3.0 %project.5 = (f32[192,384]{1,0:T(8,128)S(1)}, f32[192,384]{1,0:T(8,128)S(1)}) custom-call(bf16[96,1024]{1,0:T(8,128)(2,1)S(1)} %collective-permute-done.5.own_block, bf16[96,1024]{1,0:T(8,128)(2,1)S(1)} %collective-permute-done.6.first_block, bf16[96,1024]{1,0:T(8,128)(2,1)S(1)} %collective-permute-done.7.second_block, ...), custom_call_target="tpu_custom_call" | custom-call | flops 603979776 | bytes 3145728 | tf_op jit(solution)/shard_map/project/pallas_call | solution.py:186
  56.9 3.0 %project.6 = (f32[192,384]{1,0:T(8,128)S(1)}, f32[192,384]{1,0:T(8,128)S(1)}) custom-call(bf16[96,1024]{1,0:T(8,128)(2,1)S(1)} %collective-permute-done.9.own_block, bf16[96,1024]{1,0:T(8,128)(2,1)S(1)} %collective-permute-done.10.first_block, bf16[96,1024]{1,0:T(8,128)(2,1)S(1)} %collective-permute-done.11.second_block, ...), custom_call_target="tpu_custom_call" | custom-call | flops 603979776 | bytes 3145728 | tf_op jit(solution)/shard_map/project/pallas_call | solution.py:186
  60.0 3.0 %project.7 = (f32[192,384]{1,0:T(8,128)S(1)}, f32[192,384]{1,0:T(8,128)S(1)}) custom-call(bf16[96,1024]{1,0:T(8,128)(2,1)S(1)} %collective-permute-done.13.own_block, bf16[96,1024]{1,0:T(8,128)(2,1)S(1)} %collective-permute-done.14.first_block, bf16[96,1024]{1,0:T(8,128)(2,1)S(1)} %collective-permute-done.15.second_block, ...), custom_call_target="tpu_custom_call" | custom-call | flops 603979776 | bytes 3145728 | tf_op jit(solution)/shard_map/project/pallas_call | solution.py:186
  64.9 1.9 %head.1 = bf16[384,256]{1,0:T(8,128)(2,1)} custom-call(f32[208,384]{1,0:T(8,128)S(1)} %get-tuple-element.23.own_0, f32[192,384]{1,0:T(8,128)S(1)} %get-tuple-element.25.own_1, f32[192,384]{1,0:T(8,128)S(1)} %get-tuple-element.27.own_2, f32[192,384]{1,0:T(8,128)S(1)} %get-tuple-element.29.own_3, f32[208,384]{1,0:T(8,128)S(1)} %collective-permute-done.17.got_0, ...), custom_call_target="tpu_custom_call" | custom-call | tf_op jit(solution)/shard_map/head/pallas_call | solution.py:236
  (32 shorter events, 6.6 us)
Async XLA Ops:
  0.6 45.6 %collective-permute-start.4 = (bf16[384,4096]{1,0:T(8,128)(2,1)}, bf16[384,4096]{1,0:T(8,128)(2,1)S(1)}, u32[]{:S(2)}, u32[]{:S(2)}) collective-permute-start(bf16[384,4096]{1,0:T(8,128)(2,1)} %rest_0_.5), channel_id=1, source_target_pairs={{0,1},{1,0},{2,3},{3,2},{4,5},{5,4},{6,7},{7,6},{8,9},{9,8},{10,11... | collective-permute-start | bytes 9437192 | tf_op jit(solution)/shard_map/ppermute | solution.py:94
  4.5 7.5 %collective-permute-start = (bf16[96,1024]{1,0:T(8,128)(2,1)}, bf16[96,1024]{1,0:T(8,128)(2,1)S(1)}, u32[]{:S(2)}, u32[]{:S(2)}) collective-permute-start(bf16[96,1024]{1,0:T(8,128)(2,1)} %get-tuple-element.22.own_block), channel_id=1, source_target_pairs={{0,2},{1,5},{2,0},{3,7},{4,6},{5,1},{6,4},{7,3},{8,10},{9,13},{10,... | collective-permute-start | bytes 589832 | tf_op jit(solution)/shard_map/ppermute | solution.py:94
  7.1 5.9 %collective-permute-start.1 = (bf16[96,1024]{1,0:T(8,128)(2,1)}, bf16[96,1024]{1,0:T(8,128)(2,1)S(1)}, u32[]{:S(2)}, u32[]{:S(2)}) collective-permute-start(bf16[96,1024]{1,0:T(8,128)(2,1)} %get-tuple-element.22.own_block), channel_id=1, source_target_pairs={{0,4},{1,3},{2,6},{3,1},{4,0},{5,7},{6,2},{7,5},{8,12},{9,11},{10,... | collective-permute-start | bytes 589832 | tf_op jit(solution)/shard_map/ppermute | solution.py:94
  8.6 8.8 %collective-permute-start.5 = (bf16[96,1024]{1,0:T(8,128)(2,1)}, bf16[96,1024]{1,0:T(8,128)(2,1)S(1)}, u32[]{:S(2)}, u32[]{:S(2)}) collective-permute-start(bf16[96,1024]{1,0:T(8,128)(2,1)} %get-tuple-element.22.own_block), channel_id=1, source_target_pairs={{0,8},{1,9},{2,10},{3,11},{4,12},{5,13},{6,14},{7,15},{8,16},{9,17... | collective-permute-start | bytes 589832 | tf_op jit(solution)/shard_map/ppermute | solution.py:94
  17.5 6.2 %collective-permute-start.2 = (bf16[96,1024]{1,0:T(8,128)(2,1)S(1)}, bf16[96,1024]{1,0:T(8,128)(2,1)S(1)}, u32[]{:S(2)}, u32[]{:S(2)}) collective-permute-start(bf16[96,1024]{1,0:T(8,128)(2,1)S(1)} %collective-permute-done.first_block), channel_id=1, source_target_pairs={{0,4},{1,3},{2,6},{3,1},{4,0},{5,7},{6,2},{7,5},{8,12},{9,11},{10,... | collective-permute-start | bytes 589832 | tf_op jit(solution)/shard_map/ppermute | solution.py:94
  18.0 5.7 %collective-permute-start.6 = (bf16[96,1024]{1,0:T(8,128)(2,1)S(1)}, bf16[96,1024]{1,0:T(8,128)(2,1)S(1)}, u32[]{:S(2)}, u32[]{:S(2)}) collective-permute-start(bf16[96,1024]{1,0:T(8,128)(2,1)S(1)} %collective-permute-done.5.own_block), channel_id=1, source_target_pairs={{0,2},{1,5},{2,0},{3,7},{4,6},{5,1},{6,4},{7,3},{8,10},{9,13},{10,... | collective-permute-start | bytes 589832 | tf_op jit(solution)/shard_map/ppermute | solution.py:94
  18.5 7.5 %collective-permute-start.9 = (bf16[96,1024]{1,0:T(8,128)(2,1)S(1)}, bf16[96,1024]{1,0:T(8,128)(2,1)S(1)}, u32[]{:S(2)}, u32[]{:S(2)}) collective-permute-start(bf16[96,1024]{1,0:T(8,128)(2,1)S(1)} %collective-permute-done.5.own_block), channel_id=1, source_target_pairs={{0,8},{1,9},{2,10},{3,11},{4,12},{5,13},{6,14},{7,15},{8,16},{9,17... | collective-permute-start | bytes 589832 | tf_op jit(solution)/shard_map/ppermute | solution.py:94
  26.0 5.7 %collective-permute-start.8 = (bf16[96,1024]{1,0:T(8,128)(2,1)S(1)}, bf16[96,1024]{1,0:T(8,128)(2,1)S(1)}, u32[]{:S(2)}, u32[]{:S(2)}) collective-permute-start(bf16[96,1024]{1,0:T(8,128)(2,1)S(1)} %collective-permute-done.6.first_block), channel_id=1, source_target_pairs={{0,4},{1,3},{2,6},{3,1},{4,0},{5,7},{6,2},{7,5},{8,12},{9,11},{10,... | collective-permute-start | bytes 589832 | tf_op jit(solution)/shard_map/ppermute | solution.py:94
  27.5 5.7 %collective-permute-start.10 = (bf16[96,1024]{1,0:T(8,128)(2,1)S(1)}, bf16[96,1024]{1,0:T(8,128)(2,1)S(1)}, u32[]{:S(2)}, u32[]{:S(2)}) collective-permute-start(bf16[96,1024]{1,0:T(8,128)(2,1)S(1)} %collective-permute-done.9.own_block), channel_id=1, source_target_pairs={{0,2},{1,5},{2,0},{3,7},{4,6},{5,1},{6,4},{7,3},{8,10},{9,13},{10,... | collective-permute-start | bytes 589832 | tf_op jit(solution)/shard_map/ppermute | solution.py:94
  29.0 7.5 %collective-permute-start.13 = (bf16[96,1024]{1,0:T(8,128)(2,1)S(1)}, bf16[96,1024]{1,0:T(8,128)(2,1)S(1)}, u32[]{:S(2)}, u32[]{:S(2)}) collective-permute-start(bf16[96,1024]{1,0:T(8,128)(2,1)S(1)} %collective-permute-done.9.own_block), channel_id=1, source_target_pairs={{0,8},{1,9},{2,10},{3,11},{4,12},{5,13},{6,14},{7,15},{8,16},{9,17... | collective-permute-start | bytes 589832 | tf_op jit(solution)/shard_map/ppermute | solution.py:94
  36.5 8.3 %collective-permute-start.14 = (bf16[96,1024]{1,0:T(8,128)(2,1)S(1)}, bf16[96,1024]{1,0:T(8,128)(2,1)S(1)}, u32[]{:S(2)}, u32[]{:S(2)}) collective-permute-start(bf16[96,1024]{1,0:T(8,128)(2,1)S(1)} %collective-permute-done.13.own_block), channel_id=1, source_target_pairs={{0,2},{1,5},{2,0},{3,7},{4,6},{5,1},{6,4},{7,3},{8,10},{9,13},{10,... | collective-permute-start | bytes 589832 | tf_op jit(solution)/shard_map/ppermute | solution.py:94
  37.0 16.3 %collective-permute-start.7 = (bf16[96,1024]{1,0:T(8,128)(2,1)S(1)}, bf16[96,1024]{1,0:T(8,128)(2,1)S(1)}, u32[]{:S(2)}, u32[]{:S(2)}) collective-permute-start(bf16[96,1024]{1,0:T(8,128)(2,1)S(1)} %collective-permute-done.5.own_block), channel_id=1, source_target_pairs={{0,4},{1,3},{2,6},{3,1},{4,0},{5,7},{6,2},{7,5},{8,12},{9,11},{10,... | collective-permute-start | bytes 589832 | tf_op jit(solution)/shard_map/ppermute | solution.py:94
  37.5 6.7 %collective-permute-start.3 = (bf16[2,1024]{1,0:T(2,128)(2,1)}, bf16[2,1024]{1,0:T(2,128)(2,1)S(1)}, u32[]{:S(2)}, u32[]{:S(2)}) collective-permute-start(bf16[2,1024]{1,0:T(2,128)(2,1)} %bitcast.8), channel_id=1, source_target_pairs={{0,2},{1,3},{2,0},{3,1},{4,6},{5,7},{6,4},{7,5},{8,10},{9,11},{10,... | collective-permute-start | bytes 12296 | tf_op jit(solution)/shard_map/ppermute | solution.py:94
  39.0 17.4 %collective-permute-start.11 = (bf16[96,1024]{1,0:T(8,128)(2,1)S(1)}, bf16[96,1024]{1,0:T(8,128)(2,1)S(1)}, u32[]{:S(2)}, u32[]{:S(2)}) collective-permute-start(bf16[96,1024]{1,0:T(8,128)(2,1)S(1)} %collective-permute-done.9.own_block), channel_id=1, source_target_pairs={{0,4},{1,3},{2,6},{3,1},{4,0},{5,7},{6,2},{7,5},{8,12},{9,11},{10,... | collective-permute-start | bytes 589832 | tf_op jit(solution)/shard_map/ppermute | solution.py:94
  44.2 12.7 %collective-permute-start.12 = (bf16[96,1024]{1,0:T(8,128)(2,1)S(1)}, bf16[96,1024]{1,0:T(8,128)(2,1)S(1)}, u32[]{:S(2)}, u32[]{:S(2)}) collective-permute-start(bf16[96,1024]{1,0:T(8,128)(2,1)S(1)} %collective-permute-done.10.first_block), channel_id=1, source_target_pairs={{0,4},{1,3},{2,6},{3,1},{4,0},{5,7},{6,2},{7,5},{8,12},{9,11},{10,... | collective-permute-start | bytes 589832 | tf_op jit(solution)/shard_map/ppermute | solution.py:94
  44.8 15.3 %collective-permute-start.15 = (bf16[96,1024]{1,0:T(8,128)(2,1)S(1)}, bf16[96,1024]{1,0:T(8,128)(2,1)S(1)}, u32[]{:S(2)}, u32[]{:S(2)}) collective-permute-start(bf16[96,1024]{1,0:T(8,128)(2,1)S(1)} %collective-permute-done.13.own_block), channel_id=1, source_target_pairs={{0,4},{1,3},{2,6},{3,1},{4,0},{5,7},{6,2},{7,5},{8,12},{9,11},{10,... | collective-permute-start | bytes 589832 | tf_op jit(solution)/shard_map/ppermute | solution.py:94
  46.3 13.8 %collective-permute-start.16 = (bf16[96,1024]{1,0:T(8,128)(2,1)S(1)}, bf16[96,1024]{1,0:T(8,128)(2,1)S(1)}, u32[]{:S(2)}, u32[]{:S(2)}) collective-permute-start(bf16[96,1024]{1,0:T(8,128)(2,1)S(1)} %collective-permute-done.14.first_block), channel_id=1, source_target_pairs={{0,4},{1,3},{2,6},{3,1},{4,0},{5,7},{6,2},{7,5},{8,12},{9,11},{10,... | collective-permute-start | bytes 589832 | tf_op jit(solution)/shard_map/ppermute | solution.py:94
  46.8 1.9 %copy-start = (bf16[384,4096]{1,0:T(8,128)(2,1)S(1)}, bf16[384,4096]{1,0:T(8,128)(2,1)}, u32[]{:S(2)}) copy-start(bf16[384,4096]{1,0:T(8,128)(2,1)} %rest_0_.5) | copy-start | bytes 9437188
  48.7 0.9 %copy-start.2 = (bf16[96,1024]{1,0:T(8,128)(2,1)S(1)}, bf16[96,1024]{1,0:T(8,128)(2,1)}, u32[]{:S(2)}) copy-start(bf16[96,1024]{1,0:T(8,128)(2,1)} %get-tuple-element.22.own_block) | copy-start | bytes 589828
  50.3 3.1 %copy-start.1 = (bf16[384,4096]{1,0:T(8,128)(2,1)S(1)}, bf16[384,4096]{1,0:T(8,128)(2,1)}, u32[]{:S(2)}) copy-start(bf16[384,4096]{1,0:T(8,128)(2,1)} %rest_0_.5) | copy-start | bytes 9437188
  53.3 11.6 %collective-permute-start.17 = (f32[208,384]{1,0:T(8,128)S(1)}, f32[208,384]{1,0:T(8,128)S(1)}, u32[]{:S(2)}, u32[]{:S(2)}) collective-permute-start(f32[208,384]{1,0:T(8,128)S(1)} %get-tuple-element.30), channel_id=1, source_target_pairs={{0,1},{1,0},{2,3},{3,2},{4,5},{5,4},{6,7},{7,6},{8,9},{9,8},{10,11... | collective-permute-start | bytes 958472 | tf_op jit(solution)/shard_map/ppermute | solution.py:94
  56.4 8.4 %collective-permute-start.18 = (f32[192,384]{1,0:T(8,128)S(1)}, f32[192,384]{1,0:T(8,128)S(1)}, u32[]{:S(2)}, u32[]{:S(2)}) collective-permute-start(f32[192,384]{1,0:T(8,128)S(1)} %get-tuple-element.31), channel_id=1, source_target_pairs={{0,1},{1,0},{2,3},{3,2},{4,5},{5,4},{6,7},{7,6},{8,9},{9,8},{10,11... | collective-permute-start | bytes 884744 | tf_op jit(solution)/shard_map/ppermute | solution.py:94
  59.9 4.9 %collective-permute-start.19 = (f32[192,384]{1,0:T(8,128)S(1)}, f32[192,384]{1,0:T(8,128)S(1)}, u32[]{:S(2)}, u32[]{:S(2)}) collective-permute-start(f32[192,384]{1,0:T(8,128)S(1)} %get-tuple-element.32), channel_id=1, source_target_pairs={{0,1},{1,0},{2,3},{3,2},{4,5},{5,4},{6,7},{7,6},{8,9},{9,8},{10,11... | collective-permute-start | bytes 884744 | tf_op jit(solution)/shard_map/ppermute | solution.py:94
  63.0 1.8 %collective-permute-start.20 = (f32[192,384]{1,0:T(8,128)S(1)}, f32[192,384]{1,0:T(8,128)S(1)}, u32[]{:S(2)}, u32[]{:S(2)}) collective-permute-start(f32[192,384]{1,0:T(8,128)S(1)} %get-tuple-element.33), channel_id=1, source_target_pairs={{0,1},{1,0},{2,3},{3,2},{4,5},{5,4},{6,7},{7,6},{8,9},{9,8},{10,11... | collective-permute-start | bytes 884744 | tf_op jit(solution)/shard_map/ppermute | solution.py:94
  (1 other events, 0.7 us)

commit v2 on v0

--- a/solution.py
+++ b/solution.py
@@ -1,6 +1,11 @@
+import functools
+import itertools
+
 import jax
 import jax.numpy as jnp
 from jax import lax
+from jax.experimental import pallas as pl
+from jax.experimental.pallas import tpu as pltpu
 from jax.sharding import PartitionSpec as P
 
 QK = 256
@@ -12,6 +17,19 @@
 adam_eps = 1e-08
 fix_first = 1.0 - (0.9**10) ** 10
 fix_second = 1.0 - (0.999**10) ** 10
+
+AXES = ("group", "inner")
+NT = (((1,), (1,)), ((), ()))
+TN = (((0,), (0,)), ((), ()))
+
+
+def adam(first_moment, second_moment, master_weight, gradient):
+    new_first = beta_first * first_moment + (1.0 - beta_first) * gradient
+    new_second = beta_second * second_moment + (1.0 - beta_second) * gradient * gradient
+    new_master = master_weight - learn_rate * (new_first / fix_first) / (
+        jnp.sqrt(new_second / fix_second) + adam_eps
+    )
+    return new_master, new_first, new_second
 
 
 def mlstm_head(sequence, projected, gate_pre, input_bias, forget_bias):
@@ -34,21 +52,10 @@
     return (numerator / jnp.maximum(jnp.abs(normalizer), 1.0)[:, None]).astype(jnp.bfloat16)
 
 
-def on_device(
-    tokens,
-    master_weight,
-    first_moment,
-    second_moment,
-    gradient,
-    gate_weight,
-    input_bias,
-    forget_bias,
+def gathered_everywhere(
+    tokens, master_weight, first_moment, second_moment, gradient, gate_weight, input_bias, forget_bias
 ):
-    new_first = beta_first * first_moment + (1.0 - beta_first) * gradient
-    new_second = beta_second * second_moment + (1.0 - beta_second) * gradient * gradient
-    new_master = master_weight - learn_rate * (new_first / fix_first) / (
-        jnp.sqrt(new_second / fix_second) + adam_eps
-    )
+    new_master, new_first, new_second = adam(first_moment, second_moment, master_weight, gradient)
     sendable = new_master.astype(jnp.bfloat16)
     secondary = lax.all_gather(sendable, "group", axis=1, tiled=True)
     projected = jnp.dot(
@@ -63,6 +70,268 @@
     )
     hidden = mlstm_head(tokens, projected, gate_pre, input_bias, forget_bias)
     return (new_master, new_first, new_second, hidden)
+
+
+NZ, NY, NX, NC = 4, 2, 2, 2
+
+
+def permutation(target):
+    pairs = []
+    for z, y, x, c in itertools.product(range(NZ), range(NY), range(NX), range(NC)):
+        to_z, to_y, to_x, to_c = target(z, y, x, c)
+        pairs.append((((z * NY + y) * NX + x) * NC + c, ((to_z * NY + to_y) * NX + to_x) * NC + to_c))
+    return pairs
+
+
+OTHER_CORE = permutation(lambda z, y, x, c: (z, y, x, 1 - c))
+OTHER_X = permutation(lambda z, y, x, c: (z, y, 1 - x, c))
+FLIP_Z = [permutation(lambda z, y, x, c, flip=flip: (z ^ flip, y, x, c)) for flip in range(NZ)]
+FIRST = permutation(lambda z, y, x, c: (z, y, 1 - x, c) if c == 0 else (z, 1 - y, x, c))
+SECOND = permutation(lambda z, y, x, c: (z, 1 - y, x, c) if c == 0 else (z, y, 1 - x, c))
+
+
+def send(block, pairs):
+    return lax.ppermute(block, AXES, pairs)
+
+
+def place():
+    group, inner = lax.axis_index("group"), lax.axis_index("inner")
+    return group // NY, group % NY, inner // NC, inner % NC
+
+
+GATE_ROWS = 16
+
+
+def adam_kernel(
+    master_ref, first_ref, second_ref, grad_ref, gate_ref, to_master, to_first, to_second, to_send, to_send_gated
+):
+    new_master, new_first, new_second = adam(
+        first_ref[...], second_ref[...], master_ref[...], grad_ref[...]
+    )
+    to_master[...] = new_master
+    to_first[...] = new_first
+    to_second[...] = new_second
+    rows = new_master.shape[0]
+    at = pl.ds(pl.multiple_of(pl.program_id(0) * rows, 16), rows)
+    to_send[at] = new_master.astype(jnp.bfloat16)
+    to_send_gated[at] = new_master.astype(jnp.bfloat16)
+
+    @pl.when(pl.program_id(0) == 0)
+    def _():
+        gate = gate_ref[...]
+        pad = jnp.zeros((GATE_ROWS - gate.shape[0], gate.shape[1]), gate.dtype)
+        to_send_gated[to_send.shape[0] :] = jnp.concatenate([gate, pad], axis=0)
+
+
+def adam_step(master, first, second, grad, gate):
+    columns, rows = master.shape
+    steps = 2
+    spec = pl.BlockSpec((columns // steps, rows), lambda i: (i, 0))
+    wide = jax.ShapeDtypeStruct(master.shape, jnp.float32)
+    sent = [(columns, rows), (columns + GATE_ROWS, rows)]
+    return pl.pallas_call(
+        adam_kernel,
+        grid=(steps,),
+        in_specs=[spec] * 4 + [pl.BlockSpec(gate.shape, lambda i: (0, 0))],
+        out_specs=[spec] * 3 + [pl.BlockSpec(shape, lambda i: (0, 0)) for shape in sent],
+        out_shape=[wide] * 3 + [jax.ShapeDtypeStruct(shape, jnp.bfloat16) for shape in sent],
+        name="adam",
+    )(master, first, second, grad, gate)
+
+
+VMEM = pl.BlockSpec(memory_space=pltpu.VMEM)
+SMEM = pl.BlockSpec(memory_space=pltpu.SMEM)
+HBM = pl.BlockSpec(memory_space=pltpu.HBM)
+ROOM = pltpu.CompilerParams(vmem_limit_bytes=20 * 2**20)
+
+def hold_kernel(tokens, gated, held, held_gated, sems):
+    copies = [
+        pltpu.make_async_copy(source, target, sems.at[n])
+        for n, (source, target) in enumerate(((tokens, held), (gated, held_gated)))
+    ]
+    for copy in copies:
+        copy.start()
+    for copy in copies:
+        copy.wait()
+
+
+def hold(tokens, gated):
+    return pl.pallas_call(
+        hold_kernel,
+        in_specs=[HBM] * 2,
+        out_specs=[VMEM] * 2,
+        out_shape=[jax.ShapeDtypeStruct(array.shape, array.dtype) for array in (tokens, gated)],
+        scratch_shapes=[pltpu.SemaphoreType.DMA((2,))],
+        compiler_params=ROOM,
+        cost_estimate=pl.CostEstimate(flops=0, bytes_accessed=31457280, transcendentals=0),
+        name="hold",
+    )(tokens, gated)
+
+
+def row_block(its_x, its_c, depth):
+    return pl.ds(pl.multiple_of((its_x * NC + its_c) * depth, depth), depth)
+
+
+def project_kernel(columns, gated, *refs):
+    blocks, (tokens, tokens_other, out_own, out_send, stack) = refs[:-5], refs[-5:]
+    _, y, x, c = place()
+    depth = blocks[0].shape[1]
+    swap = c == 0
+    spots = (
+        (0, y),
+        (jnp.where(swap, 1, 0), jnp.where(swap, y, 1 - y)),
+        (jnp.where(swap, 0, 1), jnp.where(swap, 1 - y, y)),
+        (1, 1 - y),
+    )
+    for block, (side, its_y) in zip(blocks, spots):
+        stack[side, pl.ds(pl.multiple_of(its_y * columns, 16), columns)] = block[:columns]
+    if len(blocks) == 3:
+        side, its_y = spots[3]
+        stack[side, pl.ds(pl.multiple_of(its_y * columns, 16), columns)] = jnp.zeros(
+            (columns, depth), jnp.bfloat16
+        )
+    if gated:
+        _, first, second = (block[columns:] for block in blocks[:3])
+        stack[0, NY * columns :] = blocks[0][columns:]
+        stack[1, NY * columns :] = jnp.where(swap, first, second)
+    for source, out in ((tokens_other, out_send), (tokens, out_own)):
+        parts = [
+            lax.dot_general(
+                stack[side], source[:, row_block(its_x, c, depth)], NT, preferred_element_type=jnp.float32
+            )
+            for side, its_x in enumerate((x, 1 - x))
+        ]
+        out[...] = parts[0] + parts[1]
+
+
+def project(columns, blocks, tokens, tokens_other):
+    its_rows, depth = blocks[0].shape
+    gated = its_rows > columns
+    rows = NY * columns + (GATE_ROWS if gated else 0)
+    sequence = tokens.shape[0]
+    out = jax.ShapeDtypeStruct((rows, sequence), jnp.float32)
+    return pl.pallas_call(
+        functools.partial(project_kernel, columns, gated),
+        in_specs=[VMEM] * (len(blocks) + 2),
+        out_specs=[VMEM] * 2,
+        out_shape=[out, out],
+        scratch_shapes=[pltpu.VMEM((NX, rows, depth), jnp.bfloat16)],
+        compiler_params=ROOM,
+        cost_estimate=pl.CostEstimate(
+            flops=2 * 2 * NX * rows * depth * sequence, bytes_accessed=8 * sequence * depth, transcendentals=0
+        ),
+        name="project",
+    )(*blocks, tokens, tokens_other)
+
+
+def decay_kernel(own, got, input_bias, forget_bias, out):
+    rows, sequence = own.shape
+    gate_pre = own[rows - GATE_ROWS : rows - 8] + got[rows - GATE_ROWS : rows - 8]
+    input_gate = gate_pre[0:1] + input_bias[0]
+    cumulative = jax.nn.log_sigmoid(gate_pre[1:2] + forget_bias[0])
+    lane = lax.broadcasted_iota(jnp.int32, (1, sequence), 1)
+    step = 1
+    while step < sequence:
+        cumulative = cumulative + jnp.where(lane >= step, pltpu.roll(cumulative, step, 1), 0.0)
+        step *= 2
+    source = jnp.broadcast_to(input_gate - cumulative, (8, sequence)).T[:, 0:1]
+    to_t = lax.broadcasted_iota(jnp.int32, (sequence, sequence), 1)
+    from_s = lax.broadcasted_iota(jnp.int32, (sequence, sequence), 0)
+    out[...] = jnp.exp(jnp.where(from_s <= to_t, cumulative + source, -jnp.inf))
+
+
+def decay_matrix(own, got, input_bias, forget_bias):
+    sequence = own.shape[1]
+    return pl.pallas_call(
+        decay_kernel,
+        in_specs=[VMEM, VMEM, SMEM, SMEM],
+        out_specs=VMEM,
+        out_shape=jax.ShapeDtypeStruct((sequence, sequence), jnp.float32),
+        compiler_params=ROOM,
+        name="decay",
+    )(own, got, input_bias, forget_bias)
+
+
+def head_kernel(columns, offsets, *refs):
+    count = len(offsets)
+    own, got = refs[:count], refs[count : 2 * count]
+    last, last_other, tokens, decay, out, projected = refs[2 * count :]
+    z, y, x, c = place()
+    width, depth = last.shape
+    for mine, theirs, offset in zip(own, got, offsets):
+        at = pl.multiple_of(lax.bitwise_xor(z, offset) * columns, 16)
+        projected[pl.ds(at, columns)] = mine[:columns] + theirs[:columns]
+    rest = lax.dot_general(
+        last[...], tokens[:, row_block(1 - x, c, depth)], NT, preferred_element_type=jnp.float32
+    ) + lax.dot_general(
+        last_other[...], tokens[:, row_block(1 - x, 1 - c, depth)], NT, preferred_element_type=jnp.float32
+    )
+    at = pl.multiple_of(lax.bitwise_xor(z, offsets[-1]) * columns + (1 - y) * width, 16)
+    projected[pl.ds(at, width)] += rest
+    query, key, value = (projected[n * QK : (n + 1) * QK].astype(jnp.bfloat16) for n in range(3))
+    scores = lax.dot_general(key, query, TN, preferred_element_type=jnp.float32) * QK ** (-0.5)
+    weighted = scores * decay[...]
+    normalizer = jnp.sum(weighted, axis=0, keepdims=True)
+    numerator = jnp.dot(value, weighted.astype(jnp.bfloat16), preferred_element_type=jnp.float32)
+    out[...] = (numerator / jnp.maximum(jnp.abs(normalizer), 1.0)).T.astype(jnp.bfloat16)
+
+
+def head(offsets, own, got, last, last_other, tokens, decay):
+    sequence = tokens.shape[0]
+    columns = NY * last.shape[0]
+    return pl.pallas_call(
+        functools.partial(head_kernel, columns, offsets),
+        in_specs=[VMEM] * (2 * len(offsets) + 4),
+        out_specs=VMEM,
+        out_shape=jax.ShapeDtypeStruct((sequence, NZ * columns - 2 * QK), jnp.bfloat16),
+        scratch_shapes=[pltpu.VMEM((NZ * columns, sequence), jnp.float32)],
+        compiler_params=ROOM,
+        name="head",
+    )(*own, *got, last, last_other, tokens, decay)
+
+
+def after(value, *others):
+    return lax.optimization_barrier((value,) + others)[0]
+
+
+def by_links(
+    tokens, master_weight, first_moment, second_moment, gradient, gate_weight, input_bias, forget_bias
+):
+    new_master, new_first, new_second, block, gated = adam_step(
+        master_weight.T, first_moment.T, second_moment.T, gradient.T, gate_weight.T
+    )
+    columns = block.shape[0]
+    tokens_other = send(tokens, OTHER_CORE)
+    z1 = send(block, FLIP_Z[1])
+    a1 = send(gated, FIRST)
+    a2 = send(gated, SECOND)
+    z2 = send(block, FLIP_Z[2])
+    held, held_gated = hold(after(tokens, a1), gated)
+    b1 = send(z1, FIRST)
+    a3 = send(after(a1, z1, held), SECOND)
+    b2 = send(after(z1, a2, z2), SECOND)
+    z3 = send(after(block, a2), FLIP_Z[3])
+    d1 = send(after(z2, b1), FIRST)
+    b3 = send(after(b1, b2), SECOND)
+    d2 = send(after(z2, a3), SECOND)
+    own_a, part_a = project(columns, (held_gated, a1, a2, a3), held, tokens_other)
+    got_a = send(part_a, OTHER_CORE)
+    d3 = send(d1, SECOND)
+    c1 = send(after(z3, own_a), FIRST)
+    c2 = send(after(z3, own_a), SECOND)
+    own_b, part_b = project(columns, (z1, b1, b2, b3), held, tokens_other)
+    got_b = send(part_b, OTHER_CORE)
+    decay = decay_matrix(own_a, got_a, input_bias, forget_bias)
+    c3 = send(after(c1, own_b, decay), SECOND)
+    own_d, part_d = project(columns, (z2, d1, d2, d3), held, tokens_other)
+    got_d = send(part_d, OTHER_CORE)
+    own_c, part_c = project(columns, (z3, c1, c2), held, tokens_other)
+    got_c = send(part_c, OTHER_CORE)
+    c3_other = send(c3, OTHER_CORE)
+    hidden = head(
+        (0, 1, 2, 3), (own_a, own_b, own_d, own_c), (got_a, got_b, got_d, got_c), c3, c3_other, held, decay
+    )
+    return (new_master.T, new_first.T, new_second.T, hidden)
 
 
 def solution(mesh):
@@ -76,8 +345,9 @@
         P(),
         P(),
     )
+    fits = mesh.shape["group"] == NZ * NY and mesh.shape["inner"] == NX * NC
     return jax.shard_map(
-        on_device,
+        by_links if fits else gathered_everywhere,
         mesh=mesh,
         in_specs=placed,
         out_specs=(

time: 118 us -> 48.8 us (0.41)
  waiting for transfers between devices: 86.4 us -> 14.8 us
  starting transfers between devices: 0.08 us -> 18.1 us
  between operations: 15.4 us -> 2.06 us
  Pallas kernels: 0 us -> 10.8 us
  matrix products: 7.83 us -> 0 us
  blocking collectives: 5.19 us -> 0 us
  other arithmetic: 3.21 us -> 0 us
  local copies, waits for them, and re-layouts: 0.21 us -> 2.83 us
    all_gather x2 -> x0, waiting for transfers between devices: 86.3 us -> none  [the longest x1 47.7 us: on_device(): secondary = lax.all_gather(sendable, 'group', axis=1, tiled=True)]
    ppermute x0 -> x21, starting transfers between devices: none -> 18.1 us  [send(): return lax.ppermute(block, AXES, pairs)]
    ppermute x0 -> x21, waiting for transfers between devices: none -> 14.8 us  [send(): return lax.ppermute(block, AXES, pairs)]
    pallas_call x0 -> x8, Pallas kernels: none -> 10.8 us  [the longest x4 4.81 us: project(): pl.pallas_call(functools.partial(project_kernel, columns, gated), in_spec...]
    dot_general x4 -> x0, matrix products: 7.83 us -> none  [the longest x1 5.59 us: on_device(): jnp.dot(tokens, lax.all_gather(secondary, 'inner', axis=0, tiled=True), p...]
    all_gather x1 -> x0, blocking collectives: 5.19 us -> none  [on_device(): lax.all_gather(gate_weight, 'inner', axis=0, tiled=True)]
    unnamed x4 -> x6, local copies, waits for them, and re-layouts: 0.01 us -> 2.83 us
    convert_element_type x1 -> x0, other arithmetic: 2.73 us -> none  [on_device(): sendable = new_master.astype(jnp.bfloat16)]
  transfers between devices with their start and end apart: 2 -> 21, of which waited for: 2 -> 11; matrix products, arithmetic and copies ran while one was open for 1% -> 0% of each run, Pallas kernels for 0% -> 18%
where the time goes in v2:
time: 48.8 us; the launch traced here: 48.6 us
  starting transfers between devices  18.1 us (37%)
  waiting for transfers between devices  14.8 us (30%)
  Pallas kernels  10.8 us (22%)
  local copies, waits for them, and re-layouts  2.83 us (6%)
  between operations  2.06 us (4%)
    ppermute x21, starting transfers between devices, send(): return lax.ppermute(block, AXES, pairs)  18.1 us
    ppermute x21, waiting for transfers between devices, send(): return lax.ppermute(block, AXES, pairs)  14.8 us
    pallas_call x4, Pallas kernels, project(): pl.pallas_call(functools.partial(project_kernel, columns, gated), in_spec...  4.81 us
    unnamed x6, local copies, waits for them, and re-layouts  2.83 us
    pallas_call x1, Pallas kernels, adam_step(): pl.pallas_call(adam_kernel, grid=(steps,), in_specs=[spec] * 4 + [pl.Bloc...  2.6 us
    pallas_call x1, Pallas kernels, head(): pl.pallas_call(functools.partial(head_kernel, columns, offsets), in_specs...  2.1 us
  transfers between devices with their start and end apart: 21, of which 11 were waited for; matrix products, arithmetic and copies ran while one was open for 0% of the time, Pallas kernels for 18%

profile of v2, /device:TPU:0, one launch (start us, length us, event | category | flops | bytes accessed | tf_op | source)
XLA Modules:
  0.0 48.6 jit_solution(7882236397225846019)
XLA Ops:
  1.1 2.6 %adam.1 = (f32[96,1024]{1,0:T(8,128)}, f32[96,1024]{1,0:T(8,128)}, f32[96,1024]{1,0:T(8,128)}, bf16[96,1024]{1,0:T(8,128)(2,1)}, bf16[112,1024]{1,0:T(8,128)(2,1)}) custom-call(f32[96,1024]{1,0:T(8,128)} %bitcast.8, f32[96,1024]{1,0:T(8,128)} %bitcast.9, f32[96,1024]{1,0:T(8,128)} %bitcast.10, f32[96,1024]{1,0:T(8,128)} %bitcast.11, bf16[2,1024]{1,0:T(2,128)(2,1)} %bitcast.12), custom_call_target="tpu_custom_call" | custom-call | tf_op jit(solution)/shard_map/adam/pallas_call | solution.py:132
  3.8 2.6 %collective-permute-start = (bf16[112,1024]{1,0:T(8,128)(2,1)}, bf16[112,1024]{1,0:T(8,128)(2,1)S(1)}, u32[]{:S(2)}, u32[]{:S(2)}) collective-permute-start(bf16[112,1024]{1,0:T(8,128)(2,1)} %get-tuple-element.31.gated), channel_id=1, source_target_pairs={{0,2},{1,5},{2,0},{3,7},{4,6},{5,1},{6,4},{7,3},{8,10},{9,13},{10,... | collective-permute-start | bytes 688136 | tf_op jit(solution)/shard_map/ppermute | solution.py:94
  6.3 1.5 %collective-permute-start.1 = (bf16[112,1024]{1,0:T(8,128)(2,1)}, bf16[112,1024]{1,0:T(8,128)(2,1)S(1)}, u32[]{:S(2)}, u32[]{:S(2)}) collective-permute-start(bf16[112,1024]{1,0:T(8,128)(2,1)} %get-tuple-element.31.gated), channel_id=1, source_target_pairs={{0,4},{1,3},{2,6},{3,1},{4,0},{5,7},{6,2},{7,5},{8,12},{9,11},{10,... | collective-permute-start | bytes 688136 | tf_op jit(solution)/shard_map/ppermute | solution.py:94
  7.9 1.6 %collective-permute-start.2 = (bf16[96,1024]{1,0:T(8,128)(2,1)}, bf16[96,1024]{1,0:T(8,128)(2,1)S(1)}, u32[]{:S(2)}, u32[]{:S(2)}) collective-permute-start(bf16[96,1024]{1,0:T(8,128)(2,1)} %get-tuple-element.44), channel_id=1, source_target_pairs={{0,8},{1,9},{2,10},{3,11},{4,12},{5,13},{6,14},{7,15},{8,0},{9,1},... | collective-permute-start | bytes 589832 | tf_op jit(solution)/shard_map/ppermute | solution.py:94
  9.4 2.6 %collective-permute-start.6 = (bf16[96,1024]{1,0:T(8,128)(2,1)}, bf16[96,1024]{1,0:T(8,128)(2,1)S(1)}, u32[]{:S(2)}, u32[]{:S(2)}) collective-permute-start(bf16[96,1024]{1,0:T(8,128)(2,1)} %get-tuple-element.44), channel_id=1, source_target_pairs={{0,16},{1,17},{2,18},{3,19},{4,20},{5,21},{6,22},{7,23},{8,24},{9,... | collective-permute-start | bytes 589832 | tf_op jit(solution)/shard_map/ppermute | solution.py:94
  12.0 1.9 %copy-done = bf16[384,4096]{1,0:T(8,128)(2,1)S(1)} copy-done((bf16[384,4096]{1,0:T(8,128)(2,1)S(1)}, bf16[384,4096]{1,0:T(8,128)(2,1)}, u32[]{:S(2)}) %copy-start) | copy-done | bytes 3145752
  13.9 0.9 %copy-done.1 = bf16[112,1024]{1,0:T(8,128)(2,1)S(1)} copy-done((bf16[112,1024]{1,0:T(8,128)(2,1)S(1)}, bf16[112,1024]{1,0:T(8,128)(2,1)}, u32[]{:S(2)}) %copy-start.1) | copy-done | bytes 229400
  15.4 3.5 %collective-permute-done.2.refs_0_ = bf16[96,1024]{1,0:T(8,128)(2,1)S(1)} collective-permute-done((bf16[96,1024]{1,0:T(8,128)(2,1)}, bf16[96,1024]{1,0:T(8,128)(2,1)S(1)}, u32[]{:S(2)}, u32[]{:S(2)}) %collective-permute-start.2) | collective-permute-done | bytes 196640 | tf_op jit(solution)/shard_map/ppermute | solution.py:94
  19.8 1.5 %collective-permute-done.6.refs_0_ = bf16[96,1024]{1,0:T(8,128)(2,1)S(1)} collective-permute-done((bf16[96,1024]{1,0:T(8,128)(2,1)}, bf16[96,1024]{1,0:T(8,128)(2,1)S(1)}, u32[]{:S(2)}, u32[]{:S(2)}) %collective-permute-start.6) | collective-permute-done | bytes 196640 | tf_op jit(solution)/shard_map/ppermute | solution.py:94
  21.8 2.5 %collective-permute-start.12 = (bf16[96,1024]{1,0:T(8,128)(2,1)S(1)}, bf16[96,1024]{1,0:T(8,128)(2,1)S(1)}, u32[]{:S(2)}, u32[]{:S(2)}) collective-permute-start(bf16[96,1024]{1,0:T(8,128)(2,1)S(1)} %copy-done.2), channel_id=1, source_target_pairs={{0,24},{1,25},{2,26},{3,27},{4,28},{5,29},{6,30},{7,31},{8,16},{9,... | collective-permute-start | bytes 589832 | tf_op jit(solution)/shard_map/ppermute | solution.py:94
  24.2 2.7 %collective-permute-done.5.refs_1_ = bf16[96,1024]{1,0:T(8,128)(2,1)S(1)} collective-permute-done((bf16[96,1024]{1,0:T(8,128)(2,1)S(1)}, bf16[96,1024]{1,0:T(8,128)(2,1)S(1)}, u32[]{:S(2)}, u32[]{:S(2)}) %collective-permute-start.5) | collective-permute-done | bytes 196640 | tf_op jit(solution)/shard_map/ppermute | solution.py:94
  27.5 1.4 %collective-permute-done.7.refs_2_ = bf16[96,1024]{1,0:T(8,128)(2,1)S(1)} collective-permute-done((bf16[96,1024]{1,0:T(8,128)(2,1)S(1)}, bf16[96,1024]{1,0:T(8,128)(2,1)S(1)}, u32[]{:S(2)}, u32[]{:S(2)}) %collective-permute-start.7) | collective-permute-done | bytes 196640 | tf_op jit(solution)/shard_map/ppermute | solution.py:94
  29.4 1.2 %project.4 = (f32[208,384]{1,0:T(8,128)S(1)}, f32[208,384]{1,0:T(8,128)S(1)}) custom-call(bf16[112,1024]{1,0:T(8,128)(2,1)S(1)} %get-tuple-element.33.refs_0_, bf16[112,1024]{1,0:T(8,128)(2,1)S(1)} %collective-permute-done.refs_1_, bf16[112,1024]{1,0:T(8,128)(2,1)S(1)} %collective-permute-done.1.refs_2_, ...), custom_call_target="tpu_custom_call" | custom-call | flops 654311424 | bytes 3145728 | tf_op jit(solution)/shard_map/project/pallas_call | solution.py:213
  31.0 1.7 %collective-permute-start.10 = (bf16[96,1024]{1,0:T(8,128)(2,1)S(1)}, bf16[96,1024]{1,0:T(8,128)(2,1)S(1)}, u32[]{:S(2)}, u32[]{:S(2)}) collective-permute-start(bf16[96,1024]{1,0:T(8,128)(2,1)S(1)} %collective-permute-done.6.refs_0_), channel_id=1, source_target_pairs={{0,4},{1,3},{2,6},{3,1},{4,0},{5,7},{6,2},{7,5},{8,12},{9,11},{10,... | collective-permute-start | bytes 589832 | tf_op jit(solution)/shard_map/ppermute | solution.py:94
  32.7 0.8 %collective-permute-done.9.refs_1_ = bf16[96,1024]{1,0:T(8,128)(2,1)S(1)} collective-permute-done((bf16[96,1024]{1,0:T(8,128)(2,1)S(1)}, bf16[96,1024]{1,0:T(8,128)(2,1)S(1)}, u32[]{:S(2)}, u32[]{:S(2)}) %collective-permute-start.9) | collective-permute-done | bytes 196640 | tf_op jit(solution)/shard_map/ppermute | solution.py:94
  33.5 1.7 %collective-permute-done.8.refs_3_ = bf16[96,1024]{1,0:T(8,128)(2,1)S(1)} collective-permute-done((bf16[96,1024]{1,0:T(8,128)(2,1)S(1)}, bf16[96,1024]{1,0:T(8,128)(2,1)S(1)}, u32[]{:S(2)}, u32[]{:S(2)}) %collective-permute-start.8) | collective-permute-done | bytes 196640 | tf_op jit(solution)/shard_map/ppermute | solution.py:94
  36.9 1.2 %project.5 = (f32[192,384]{1,0:T(8,128)S(1)}, f32[192,384]{1,0:T(8,128)S(1)}) custom-call(bf16[96,1024]{1,0:T(8,128)(2,1)S(1)} %collective-permute-done.2.refs_0_, bf16[96,1024]{1,0:T(8,128)(2,1)S(1)} %collective-permute-done.5.refs_1_, bf16[96,1024]{1,0:T(8,128)(2,1)S(1)} %collective-permute-done.7.refs_2_, ...), custom_call_target="tpu_custom_call" | custom-call | flops 603979776 | bytes 3145728 | tf_op jit(solution)/shard_map/project/pallas_call | solution.py:213
  38.2 0.8 %decay.1.refs_11_ = f32[384,384]{1,0:T(8,128)S(1)} custom-call(f32[208,384]{1,0:T(8,128)S(1)} %get-tuple-element.37.own.refs_0_, f32[208,384]{1,0:T(8,128)S(1)} %collective-permute-done.15.got.refs_4_, f32[1]{0:T(128)S(6)} %copy.12.input_bias, f32[1]{0:T(128)S(6)} %copy.13.forget_bias), custom_call_target="tpu_custom_call" | custom-call | tf_op jit(solution)/shard_map/decay/pallas_call | solution.py:245
  39.0 1.8 %collective-permute-start.19 = (bf16[96,1024]{1,0:T(8,128)(2,1)S(1)}, bf16[96,1024]{1,0:T(8,128)(2,1)S(1)}, u32[]{:S(2)}, u32[]{:S(2)}) collective-permute-start(bf16[96,1024]{1,0:T(8,128)(2,1)S(1)} %collective-permute-done.13.refs_1_), channel_id=1, source_target_pairs={{0,4},{1,3},{2,6},{3,1},{4,0},{5,7},{6,2},{7,5},{8,12},{9,11},{10,... | collective-permute-start | bytes 589832 | tf_op jit(solution)/shard_map/ppermute | solution.py:94
  40.9 1.2 %project.6 = (f32[192,384]{1,0:T(8,128)S(1)}, f32[192,384]{1,0:T(8,128)S(1)}) custom-call(bf16[96,1024]{1,0:T(8,128)(2,1)S(1)} %collective-permute-done.6.refs_0_, bf16[96,1024]{1,0:T(8,128)(2,1)S(1)} %collective-permute-done.9.refs_1_, bf16[96,1024]{1,0:T(8,128)(2,1)S(1)} %collective-permute-done.10.refs_2_, ...), custom_call_target="tpu_custom_call" | custom-call | flops 603979776 | bytes 3145728 | tf_op jit(solution)/shard_map/project/pallas_call | solution.py:213
  42.1 0.8 %collective-permute-done.14.refs_2_ = bf16[96,1024]{1,0:T(8,128)(2,1)S(1)} collective-permute-done((bf16[96,1024]{1,0:T(8,128)(2,1)S(1)}, bf16[96,1024]{1,0:T(8,128)(2,1)S(1)}, u32[]{:S(2)}, u32[]{:S(2)}) %collective-permute-start.14) | collective-permute-done | bytes 196640 | tf_op jit(solution)/shard_map/ppermute | solution.py:94
  43.0 1.2 %project.7 = (f32[192,384]{1,0:T(8,128)S(1)}, f32[192,384]{1,0:T(8,128)S(1)}) custom-call(bf16[96,1024]{1,0:T(8,128)(2,1)S(1)} %collective-permute-done.12.refs_0_, bf16[96,1024]{1,0:T(8,128)(2,1)S(1)} %collective-permute-done.13.refs_1_, bf16[96,1024]{1,0:T(8,128)(2,1)S(1)} %collective-permute-done.14.refs_2_, ...), custom_call_target="tpu_custom_call" | custom-call | flops 603979776 | bytes 3145728 | tf_op jit(solution)/shard_map/project/pallas_call | solution.py:213
  44.2 0.8 %collective-permute-done.19.refs_8_ = bf16[96,1024]{1,0:T(8,128)(2,1)S(1)} collective-permute-done((bf16[96,1024]{1,0:T(8,128)(2,1)S(1)}, bf16[96,1024]{1,0:T(8,128)(2,1)S(1)}, u32[]{:S(2)}, u32[]{:S(2)}) %collective-permute-start.19) | collective-permute-done | bytes 196640 | tf_op jit(solution)/shard_map/ppermute | solution.py:94
  46.5 2.1 %head.1 = bf16[384,256]{1,0:T(8,128)(2,1)} custom-call(f32[208,384]{1,0:T(8,128)S(1)} %get-tuple-element.37.own.refs_0_, f32[192,384]{1,0:T(8,128)S(1)} %get-tuple-element.40.refs_1_, f32[192,384]{1,0:T(8,128)S(1)} %get-tuple-element.43.refs_2_, f32[192,384]{1,0:T(8,128)S(1)} %get-tuple-element.46.refs_3_, ...), custom_call_target="tpu_custom_call" | custom-call | tf_op jit(solution)/shard_map/head/pallas_call | solution.py:282
  (32 shorter events, 6.0 us)
Async XLA Ops:
  0.6 28.8 %collective-permute-start.4 = (bf16[384,4096]{1,0:T(8,128)(2,1)}, bf16[384,4096]{1,0:T(8,128)(2,1)S(1)}, u32[]{:S(2)}, u32[]{:S(2)}) collective-permute-start(bf16[384,4096]{1,0:T(8,128)(2,1)} %tokens), channel_id=1, source_target_pairs={{0,1},{1,0},{2,3},{3,2},{4,5},{5,4},{6,7},{7,6},{8,9},{9,8},{10,11... | collective-permute-start | bytes 9437192 | tf_op jit(solution)/shard_map/ppermute | solution.py:94
  3.8 8.3 %collective-permute-start = (bf16[112,1024]{1,0:T(8,128)(2,1)}, bf16[112,1024]{1,0:T(8,128)(2,1)S(1)}, u32[]{:S(2)}, u32[]{:S(2)}) collective-permute-start(bf16[112,1024]{1,0:T(8,128)(2,1)} %get-tuple-element.31.gated), channel_id=1, source_target_pairs={{0,2},{1,5},{2,0},{3,7},{4,6},{5,1},{6,4},{7,3},{8,10},{9,13},{10,... | collective-permute-start | bytes 688136 | tf_op jit(solution)/shard_map/ppermute | solution.py:94
  6.3 14.9 %collective-permute-start.1 = (bf16[112,1024]{1,0:T(8,128)(2,1)}, bf16[112,1024]{1,0:T(8,128)(2,1)S(1)}, u32[]{:S(2)}, u32[]{:S(2)}) collective-permute-start(bf16[112,1024]{1,0:T(8,128)(2,1)} %get-tuple-element.31.gated), channel_id=1, source_target_pairs={{0,4},{1,3},{2,6},{3,1},{4,0},{5,7},{6,2},{7,5},{8,12},{9,11},{10,... | collective-permute-start | bytes 688136 | tf_op jit(solution)/shard_map/ppermute | solution.py:94
  7.9 11.0 %collective-permute-start.2 = (bf16[96,1024]{1,0:T(8,128)(2,1)}, bf16[96,1024]{1,0:T(8,128)(2,1)S(1)}, u32[]{:S(2)}, u32[]{:S(2)}) collective-permute-start(bf16[96,1024]{1,0:T(8,128)(2,1)} %get-tuple-element.44), channel_id=1, source_target_pairs={{0,8},{1,9},{2,10},{3,11},{4,12},{5,13},{6,14},{7,15},{8,0},{9,1},... | collective-permute-start | bytes 589832 | tf_op jit(solution)/shard_map/ppermute | solution.py:94
  9.4 11.8 %collective-permute-start.6 = (bf16[96,1024]{1,0:T(8,128)(2,1)}, bf16[96,1024]{1,0:T(8,128)(2,1)S(1)}, u32[]{:S(2)}, u32[]{:S(2)}) collective-permute-start(bf16[96,1024]{1,0:T(8,128)(2,1)} %get-tuple-element.44), channel_id=1, source_target_pairs={{0,16},{1,17},{2,18},{3,19},{4,20},{5,21},{6,22},{7,23},{8,24},{9,... | collective-permute-start | bytes 589832 | tf_op jit(solution)/shard_map/ppermute | solution.py:94
  12.0 1.9 %copy-start = (bf16[384,4096]{1,0:T(8,128)(2,1)S(1)}, bf16[384,4096]{1,0:T(8,128)(2,1)}, u32[]{:S(2)}) copy-start(bf16[384,4096]{1,0:T(8,128)(2,1)} %tokens) | copy-start | bytes 9437188
  13.9 0.9 %copy-start.1 = (bf16[112,1024]{1,0:T(8,128)(2,1)S(1)}, bf16[112,1024]{1,0:T(8,128)(2,1)}, u32[]{:S(2)}) copy-start(bf16[112,1024]{1,0:T(8,128)(2,1)} %get-tuple-element.31.gated) | copy-start | bytes 688132
  14.9 6.9 %copy-start.2 = (bf16[96,1024]{1,0:T(8,128)(2,1)S(1)}, bf16[96,1024]{1,0:T(8,128)(2,1)}, u32[]{:S(2)}) copy-start(bf16[96,1024]{1,0:T(8,128)(2,1)} %get-tuple-element.44) | copy-start | bytes 589828
  18.9 10.5 %collective-permute-start.3 = (bf16[112,1024]{1,0:T(8,128)(2,1)S(1)}, bf16[112,1024]{1,0:T(8,128)(2,1)S(1)}, u32[]{:S(2)}, u32[]{:S(2)}) collective-permute-start(bf16[112,1024]{1,0:T(8,128)(2,1)S(1)} %collective-permute-done.refs_1_), channel_id=1, source_target_pairs={{0,4},{1,3},{2,6},{3,1},{4,0},{5,7},{6,2},{7,5},{8,12},{9,11},{10,... | collective-permute-start | bytes 688136 | tf_op jit(solution)/shard_map/ppermute | solution.py:94
  19.4 7.5 %collective-permute-start.5 = (bf16[96,1024]{1,0:T(8,128)(2,1)S(1)}, bf16[96,1024]{1,0:T(8,128)(2,1)S(1)}, u32[]{:S(2)}, u32[]{:S(2)}) collective-permute-start(bf16[96,1024]{1,0:T(8,128)(2,1)S(1)} %collective-permute-done.2.refs_0_), channel_id=1, source_target_pairs={{0,2},{1,5},{2,0},{3,7},{4,6},{5,1},{6,4},{7,3},{8,10},{9,13},{10,... | collective-permute-start | bytes 589832 | tf_op jit(solution)/shard_map/ppermute | solution.py:94
  21.3 7.6 %collective-permute-start.7 = (bf16[96,1024]{1,0:T(8,128)(2,1)S(1)}, bf16[96,1024]{1,0:T(8,128)(2,1)S(1)}, u32[]{:S(2)}, u32[]{:S(2)}) collective-permute-start(bf16[96,1024]{1,0:T(8,128)(2,1)S(1)} %collective-permute-done.2.refs_0_), channel_id=1, source_target_pairs={{0,4},{1,3},{2,6},{3,1},{4,0},{5,7},{6,2},{7,5},{8,12},{9,11},{10,... | collective-permute-start | bytes 589832 | tf_op jit(solution)/shard_map/ppermute | solution.py:94
  21.8 8.9 %collective-permute-start.12 = (bf16[96,1024]{1,0:T(8,128)(2,1)S(1)}, bf16[96,1024]{1,0:T(8,128)(2,1)S(1)}, u32[]{:S(2)}, u32[]{:S(2)}) collective-permute-start(bf16[96,1024]{1,0:T(8,128)(2,1)S(1)} %copy-done.2), channel_id=1, source_target_pairs={{0,24},{1,25},{2,26},{3,27},{4,28},{5,29},{6,30},{7,31},{8,16},{9,... | collective-permute-start | bytes 589832 | tf_op jit(solution)/shard_map/ppermute | solution.py:94
  26.9 6.6 %collective-permute-start.9 = (bf16[96,1024]{1,0:T(8,128)(2,1)S(1)}, bf16[96,1024]{1,0:T(8,128)(2,1)S(1)}, u32[]{:S(2)}, u32[]{:S(2)}) collective-permute-start(bf16[96,1024]{1,0:T(8,128)(2,1)S(1)} %collective-permute-done.6.refs_0_), channel_id=1, source_target_pairs={{0,2},{1,5},{2,0},{3,7},{4,6},{5,1},{6,4},{7,3},{8,10},{9,13},{10,... | collective-permute-start | bytes 589832 | tf_op jit(solution)/shard_map/ppermute | solution.py:94
  28.9 6.4 %collective-permute-start.8 = (bf16[96,1024]{1,0:T(8,128)(2,1)S(1)}, bf16[96,1024]{1,0:T(8,128)(2,1)S(1)}, u32[]{:S(2)}, u32[]{:S(2)}) collective-permute-start(bf16[96,1024]{1,0:T(8,128)(2,1)S(1)} %collective-permute-done.5.refs_1_), channel_id=1, source_target_pairs={{0,4},{1,3},{2,6},{3,1},{4,0},{5,7},{6,2},{7,5},{8,12},{9,11},{10,... | collective-permute-start | bytes 589832 | tf_op jit(solution)/shard_map/ppermute | solution.py:94
  30.6 7.5 %collective-permute-start.15 = (f32[208,384]{1,0:T(8,128)S(1)}, f32[208,384]{1,0:T(8,128)S(1)}, u32[]{:S(2)}, u32[]{:S(2)}) collective-permute-start(f32[208,384]{1,0:T(8,128)S(1)} %get-tuple-element.47), channel_id=1, source_target_pairs={{0,1},{1,0},{2,3},{3,2},{4,5},{5,4},{6,7},{7,6},{8,9},{9,8},{10,11... | collective-permute-start | bytes 958472 | tf_op jit(solution)/shard_map/ppermute | solution.py:94
  30.7 8.3 %collective-permute-start.13 = (bf16[96,1024]{1,0:T(8,128)(2,1)S(1)}, bf16[96,1024]{1,0:T(8,128)(2,1)S(1)}, u32[]{:S(2)}, u32[]{:S(2)}) collective-permute-start(bf16[96,1024]{1,0:T(8,128)(2,1)S(1)} %collective-permute-done.12.refs_0_), channel_id=1, source_target_pairs={{0,2},{1,5},{2,0},{3,7},{4,6},{5,1},{6,4},{7,3},{8,10},{9,13},{10,... | collective-permute-start | bytes 589832 | tf_op jit(solution)/shard_map/ppermute | solution.py:94
  31.0 9.8 %collective-permute-start.10 = (bf16[96,1024]{1,0:T(8,128)(2,1)S(1)}, bf16[96,1024]{1,0:T(8,128)(2,1)S(1)}, u32[]{:S(2)}, u32[]{:S(2)}) collective-permute-start(bf16[96,1024]{1,0:T(8,128)(2,1)S(1)} %collective-permute-done.6.refs_0_), channel_id=1, source_target_pairs={{0,4},{1,3},{2,6},{3,1},{4,0},{5,7},{6,2},{7,5},{8,12},{9,11},{10,... | collective-permute-start | bytes 589832 | tf_op jit(solution)/shard_map/ppermute | solution.py:94
  33.5 7.3 %collective-permute-start.11 = (bf16[96,1024]{1,0:T(8,128)(2,1)S(1)}, bf16[96,1024]{1,0:T(8,128)(2,1)S(1)}, u32[]{:S(2)}, u32[]{:S(2)}) collective-permute-start(bf16[96,1024]{1,0:T(8,128)(2,1)S(1)} %collective-permute-done.9.refs_1_), channel_id=1, source_target_pairs={{0,4},{1,3},{2,6},{3,1},{4,0},{5,7},{6,2},{7,5},{8,12},{9,11},{10,... | collective-permute-start | bytes 589832 | tf_op jit(solution)/shard_map/ppermute | solution.py:94
  35.2 7.7 %collective-permute-start.14 = (bf16[96,1024]{1,0:T(8,128)(2,1)S(1)}, bf16[96,1024]{1,0:T(8,128)(2,1)S(1)}, u32[]{:S(2)}, u32[]{:S(2)}) collective-permute-start(bf16[96,1024]{1,0:T(8,128)(2,1)S(1)} %collective-permute-done.12.refs_0_), channel_id=1, source_target_pairs={{0,4},{1,3},{2,6},{3,1},{4,0},{5,7},{6,2},{7,5},{8,12},{9,11},{10,... | collective-permute-start | bytes 589832 | tf_op jit(solution)/shard_map/ppermute | solution.py:94
  38.1 7.0 %collective-permute-start.16 = (f32[192,384]{1,0:T(8,128)S(1)}, f32[192,384]{1,0:T(8,128)S(1)}, u32[]{:S(2)}, u32[]{:S(2)}) collective-permute-start(f32[192,384]{1,0:T(8,128)S(1)} %get-tuple-element.48), channel_id=1, source_target_pairs={{0,1},{1,0},{2,3},{3,2},{4,5},{5,4},{6,7},{7,6},{8,9},{9,8},{10,11... | collective-permute-start | bytes 884744 | tf_op jit(solution)/shard_map/ppermute | solution.py:94
  39.0 6.1 %collective-permute-start.19 = (bf16[96,1024]{1,0:T(8,128)(2,1)S(1)}, bf16[96,1024]{1,0:T(8,128)(2,1)S(1)}, u32[]{:S(2)}, u32[]{:S(2)}) collective-permute-start(bf16[96,1024]{1,0:T(8,128)(2,1)S(1)} %collective-permute-done.13.refs_1_), channel_id=1, source_target_pairs={{0,4},{1,3},{2,6},{3,1},{4,0},{5,7},{6,2},{7,5},{8,12},{9,11},{10,... | collective-permute-start | bytes 589832 | tf_op jit(solution)/shard_map/ppermute | solution.py:94
  42.1 3.0 %collective-permute-start.17 = (f32[192,384]{1,0:T(8,128)S(1)}, f32[192,384]{1,0:T(8,128)S(1)}, u32[]{:S(2)}, u32[]{:S(2)}) collective-permute-start(f32[192,384]{1,0:T(8,128)S(1)} %get-tuple-element.49), channel_id=1, source_target_pairs={{0,1},{1,0},{2,3},{3,2},{4,5},{5,4},{6,7},{7,6},{8,9},{9,8},{10,11... | collective-permute-start | bytes 884744 | tf_op jit(solution)/shard_map/ppermute | solution.py:94
  44.2 1.6 %collective-permute-start.18 = (f32[192,384]{1,0:T(8,128)S(1)}, f32[192,384]{1,0:T(8,128)S(1)}, u32[]{:S(2)}, u32[]{:S(2)}) collective-permute-start(f32[192,384]{1,0:T(8,128)S(1)} %get-tuple-element.50), channel_id=1, source_target_pairs={{0,1},{1,0},{2,3},{3,2},{4,5},{5,4},{6,7},{7,6},{8,9},{9,8},{10,11... | collective-permute-start | bytes 884744 | tf_op jit(solution)/shard_map/ppermute | solution.py:94
  45.1 1.4 %collective-permute-start.20 = (bf16[96,1024]{1,0:T(8,128)(2,1)S(1)}, bf16[96,1024]{1,0:T(8,128)(2,1)S(1)}, u32[]{:S(2)}, u32[]{:S(2)}) collective-permute-start(bf16[96,1024]{1,0:T(8,128)(2,1)S(1)} %collective-permute-done.19.refs_8_), channel_id=1, source_target_pairs={{0,1},{1,0},{2,3},{3,2},{4,5},{5,4},{6,7},{7,6},{8,9},{9,8},{10,11... | collective-permute-start | bytes 589832 | tf_op jit(solution)/shard_map/ppermute | solution.py:94

commit v3 on v2

--- a/solution.py
+++ b/solution.py
@@ -85,7 +85,8 @@
 
 OTHER_CORE = permutation(lambda z, y, x, c: (z, y, x, 1 - c))
 OTHER_X = permutation(lambda z, y, x, c: (z, y, 1 - x, c))
-FLIP_Z = [permutation(lambda z, y, x, c, flip=flip: (z ^ flip, y, x, c)) for flip in range(NZ)]
+NEXT_Z = permutation(lambda z, y, x, c: ((z + 1) % NZ, y, x, c))
+LAST_Z = permutation(lambda z, y, x, c: ((z - 1) % NZ, y, x, c))
 FIRST = permutation(lambda z, y, x, c: (z, y, 1 - x, c) if c == 0 else (z, 1 - y, x, c))
 SECOND = permutation(lambda z, y, x, c: (z, 1 - y, x, c) if c == 0 else (z, y, 1 - x, c))
 
@@ -140,40 +141,44 @@
 
 
 VMEM = pl.BlockSpec(memory_space=pltpu.VMEM)
-SMEM = pl.BlockSpec(memory_space=pltpu.SMEM)
 HBM = pl.BlockSpec(memory_space=pltpu.HBM)
 ROOM = pltpu.CompilerParams(vmem_limit_bytes=20 * 2**20)
-
-def hold_kernel(tokens, gated, held, held_gated, sems):
+LONG = pl.CostEstimate(flops=0, bytes_accessed=30 * 2**20, transcendentals=0)
+FREE = pl.CostEstimate(flops=0, bytes_accessed=0, transcendentals=0)
+
+def hold_kernel(tokens, gated, input_bias, forget_bias, held, held_gated, biases, sems):
     copies = [
         pltpu.make_async_copy(source, target, sems.at[n])
         for n, (source, target) in enumerate(((tokens, held), (gated, held_gated)))
     ]
     for copy in copies:
         copy.start()
+    for n, bias in enumerate((input_bias, forget_bias)):
+        biases[n] = jnp.broadcast_to(bias[...], biases.shape[1:])
     for copy in copies:
         copy.wait()
 
 
-def hold(tokens, gated):
+def hold(tokens, gated, input_bias, forget_bias):
     return pl.pallas_call(
         hold_kernel,
-        in_specs=[HBM] * 2,
-        out_specs=[VMEM] * 2,
-        out_shape=[jax.ShapeDtypeStruct(array.shape, array.dtype) for array in (tokens, gated)],
+        in_specs=[HBM] * 2 + [VMEM] * 2,
+        out_specs=[VMEM] * 3,
+        out_shape=[jax.ShapeDtypeStruct(array.shape, array.dtype) for array in (tokens, gated)]
+        + [jax.ShapeDtypeStruct((2, 8, tokens.shape[0]), jnp.float32)],
         scratch_shapes=[pltpu.SemaphoreType.DMA((2,))],
         compiler_params=ROOM,
-        cost_estimate=pl.CostEstimate(flops=0, bytes_accessed=31457280, transcendentals=0),
+        cost_estimate=LONG,
         name="hold",
-    )(tokens, gated)
+    )(tokens, gated, input_bias.reshape(1, 1), forget_bias.reshape(1, 1))
 
 
 def row_block(its_x, its_c, depth):
     return pl.ds(pl.multiple_of((its_x * NC + its_c) * depth, depth), depth)
 
 
-def project_kernel(columns, gated, *refs):
-    blocks, (tokens, tokens_other, out_own, out_send, stack) = refs[:-5], refs[-5:]
+def project_kernel(columns, gathers, gated, *refs):
+    *blocks, tokens, tokens_other, out_own, out_send, stack = refs
     _, y, x, c = place()
     depth = blocks[0].shape[1]
     swap = c == 0
@@ -183,17 +188,18 @@
         (jnp.where(swap, 0, 1), jnp.where(swap, 1 - y, y)),
         (1, 1 - y),
     )
-    for block, (side, its_y) in zip(blocks, spots):
-        stack[side, pl.ds(pl.multiple_of(its_y * columns, 16), columns)] = block[:columns]
-    if len(blocks) == 3:
-        side, its_y = spots[3]
-        stack[side, pl.ds(pl.multiple_of(its_y * columns, 16), columns)] = jnp.zeros(
-            (columns, depth), jnp.bfloat16
-        )
-    if gated:
-        _, first, second = (block[columns:] for block in blocks[:3])
-        stack[0, NY * columns :] = blocks[0][columns:]
-        stack[1, NY * columns :] = jnp.where(swap, first, second)
+    gathered = [blocks[sum(gathers[:n]) :][:count] for n, count in enumerate(gathers)]
+    for n, its_blocks in enumerate(gathered):
+        for k, (side, its_y) in enumerate(spots):
+            at = pl.ds(pl.multiple_of((n * NY + its_y) * columns, 16), columns)
+            if k < len(its_blocks):
+                stack[side, at] = its_blocks[k][:columns]
+            else:
+                stack[side, at] = jnp.zeros((columns, depth), jnp.bfloat16)
+    if gated is not None:
+        own, first, second = (block[columns:] for block in gathered[gated][:3])
+        stack[0, len(gathers) * NY * columns :] = own
+        stack[1, len(gathers) * NY * columns :] = jnp.where(swap, first, second)
     for source, out in ((tokens_other, out_send), (tokens, out_own)):
         parts = [
             lax.dot_general(
@@ -204,71 +210,98 @@
         out[...] = parts[0] + parts[1]
 
 
-def project(columns, blocks, tokens, tokens_other):
-    its_rows, depth = blocks[0].shape
-    gated = its_rows > columns
-    rows = NY * columns + (GATE_ROWS if gated else 0)
+def project(columns, gathered, tokens, tokens_other, gated=None):
+    blocks = [block for its_blocks in gathered for block in its_blocks]
+    depth = blocks[0].shape[1]
+    rows = len(gathered) * NY * columns + (0 if gated is None else GATE_ROWS)
     sequence = tokens.shape[0]
     out = jax.ShapeDtypeStruct((rows, sequence), jnp.float32)
     return pl.pallas_call(
-        functools.partial(project_kernel, columns, gated),
+        functools.partial(project_kernel, columns, [len(its_blocks) for its_blocks in gathered], gated),
         in_specs=[VMEM] * (len(blocks) + 2),
         out_specs=[VMEM] * 2,
         out_shape=[out, out],
         scratch_shapes=[pltpu.VMEM((NX, rows, depth), jnp.bfloat16)],
         compiler_params=ROOM,
-        cost_estimate=pl.CostEstimate(
-            flops=2 * 2 * NX * rows * depth * sequence, bytes_accessed=8 * sequence * depth, transcendentals=0
-        ),
+        cost_estimate=FREE,
         name="project",
     )(*blocks, tokens, tokens_other)
 
 
-def decay_kernel(own, got, input_bias, forget_bias, out):
+def decay_kernel(own, got, biases, out):
     rows, sequence = own.shape
     gate_pre = own[rows - GATE_ROWS : rows - 8] + got[rows - GATE_ROWS : rows - 8]
-    input_gate = gate_pre[0:1] + input_bias[0]
-    cumulative = jax.nn.log_sigmoid(gate_pre[1:2] + forget_bias[0])
+    input_gate = gate_pre[0:1] + biases[0, 0:1]
+    cumulative = jax.nn.log_sigmoid(gate_pre[1:2] + biases[1, 0:1])
     lane = lax.broadcasted_iota(jnp.int32, (1, sequence), 1)
     step = 1
     while step < sequence:
         cumulative = cumulative + jnp.where(lane >= step, pltpu.roll(cumulative, step, 1), 0.0)
         step *= 2
-    source = jnp.broadcast_to(input_gate - cumulative, (8, sequence)).T[:, 0:1]
+    by_row = jnp.concatenate([cumulative, input_gate, jnp.zeros((6, sequence), jnp.float32)], axis=0).T
     to_t = lax.broadcasted_iota(jnp.int32, (sequence, sequence), 1)
     from_s = lax.broadcasted_iota(jnp.int32, (sequence, sequence), 0)
-    out[...] = jnp.exp(jnp.where(from_s <= to_t, cumulative + source, -jnp.inf))
-
-
-def decay_matrix(own, got, input_bias, forget_bias):
+    out[...] = jnp.exp(jnp.where(from_s <= to_t, cumulative - by_row[:, 0:1] + by_row[:, 1:2], -jnp.inf))
+
+
+def decay_matrix(own, got, biases):
     sequence = own.shape[1]
     return pl.pallas_call(
         decay_kernel,
-        in_specs=[VMEM, VMEM, SMEM, SMEM],
+        in_specs=[VMEM] * 3,
         out_specs=VMEM,
         out_shape=jax.ShapeDtypeStruct((sequence, sequence), jnp.float32),
         compiler_params=ROOM,
         name="decay",
-    )(own, got, input_bias, forget_bias)
-
-
-def head_kernel(columns, offsets, *refs):
-    count = len(offsets)
-    own, got = refs[:count], refs[count : 2 * count]
-    last, last_other, tokens, decay, out, projected = refs[2 * count :]
-    z, y, x, c = place()
+    )(own, got, biases)
+
+
+def pending_rows(offset, width):
+    z, y, _, _ = place()
+    return pl.ds(pl.multiple_of((lax.rem(z + offset, NZ) * NY + 1 - y) * width, 16), width)
+
+
+def assemble_kernel(columns, offsets, *refs):
+    own, got = refs[: len(offsets)], refs[len(offsets) : 2 * len(offsets)]
+    last, tokens, projected, pending = refs[2 * len(offsets) :]
+    z, _, x, c = place()
     width, depth = last.shape
-    for mine, theirs, offset in zip(own, got, offsets):
-        at = pl.multiple_of(lax.bitwise_xor(z, offset) * columns, 16)
-        projected[pl.ds(at, columns)] = mine[:columns] + theirs[:columns]
-    rest = lax.dot_general(
-        last[...], tokens[:, row_block(1 - x, c, depth)], NT, preferred_element_type=jnp.float32
-    ) + lax.dot_general(
-        last_other[...], tokens[:, row_block(1 - x, 1 - c, depth)], NT, preferred_element_type=jnp.float32
-    )
-    at = pl.multiple_of(lax.bitwise_xor(z, offsets[-1]) * columns + (1 - y) * width, 16)
-    projected[pl.ds(at, width)] += rest
-    query, key, value = (projected[n * QK : (n + 1) * QK].astype(jnp.bfloat16) for n in range(3))
+    at = row_block(1 - x, c, depth)
+    rest = lax.dot_general(last[...], tokens[:, at], NT, preferred_element_type=jnp.float32)
+    for mine, theirs, its_offsets in zip(own, got, offsets):
+        for n, offset in enumerate(its_offsets):
+            at = pl.multiple_of(lax.rem(z + offset, NZ) * columns, 16)
+            rows = slice(n * columns, (n + 1) * columns)
+            projected[pl.ds(at, columns)] = (mine[rows] + theirs[rows]).astype(jnp.bfloat16)
+    _, y, _, _ = place()
+    rows = pl.ds(pl.multiple_of((len(offsets[-1]) - 1) * columns + (1 - y) * width, 16), width)
+    pending[...] = own[-1][rows] + got[-1][rows] + rest
+
+
+def assemble(offsets, own, got, last, tokens):
+    sequence = tokens.shape[0]
+    width = last.shape[0]
+    return pl.pallas_call(
+        functools.partial(assemble_kernel, NY * width, offsets),
+        in_specs=[VMEM] * (2 * len(offsets) + 2),
+        out_specs=[VMEM] * 2,
+        out_shape=[
+            jax.ShapeDtypeStruct((NZ * NY * width, sequence), jnp.bfloat16),
+            jax.ShapeDtypeStruct((width, sequence), jnp.float32),
+        ],
+        compiler_params=ROOM,
+        name="assemble",
+    )(*own, *got, last, tokens)
+
+
+def head_kernel(offset, assembled, pending, last_other, tokens, decay, out, projected):
+    _, _, x, c = place()
+    width, depth = last_other.shape
+    at = row_block(1 - x, 1 - c, depth)
+    rest = lax.dot_general(last_other[...], tokens[:, at], NT, preferred_element_type=jnp.float32)
+    projected[...] = assembled[...]
+    projected[pending_rows(offset, width)] = (pending[...] + rest).astype(jnp.bfloat16)
+    query, key, value = (projected[n * QK : (n + 1) * QK] for n in range(3))
     scores = lax.dot_general(key, query, TN, preferred_element_type=jnp.float32) * QK ** (-0.5)
     weighted = scores * decay[...]
     normalizer = jnp.sum(weighted, axis=0, keepdims=True)
@@ -276,18 +309,17 @@
     out[...] = (numerator / jnp.maximum(jnp.abs(normalizer), 1.0)).T.astype(jnp.bfloat16)
 
 
-def head(offsets, own, got, last, last_other, tokens, decay):
-    sequence = tokens.shape[0]
-    columns = NY * last.shape[0]
-    return pl.pallas_call(
-        functools.partial(head_kernel, columns, offsets),
-        in_specs=[VMEM] * (2 * len(offsets) + 4),
+def head(offset, assembled, pending, last_other, tokens, decay):
+    columns, sequence = assembled.shape
+    return pl.pallas_call(
+        functools.partial(head_kernel, offset),
+        in_specs=[VMEM] * 5,
         out_specs=VMEM,
-        out_shape=jax.ShapeDtypeStruct((sequence, NZ * columns - 2 * QK), jnp.bfloat16),
-        scratch_shapes=[pltpu.VMEM((NZ * columns, sequence), jnp.float32)],
+        out_shape=jax.ShapeDtypeStruct((sequence, columns - 2 * QK), jnp.bfloat16),
+        scratch_shapes=[pltpu.VMEM(assembled.shape, jnp.bfloat16)],
         compiler_params=ROOM,
         name="head",
-    )(*own, *got, last, last_other, tokens, decay)
+    )(assembled, pending, last_other, tokens, decay)
 
 
 def after(value, *others):
@@ -302,35 +334,36 @@
     )
     columns = block.shape[0]
     tokens_other = send(tokens, OTHER_CORE)
-    z1 = send(block, FLIP_Z[1])
-    a1 = send(gated, FIRST)
-    a2 = send(gated, SECOND)
-    z2 = send(block, FLIP_Z[2])
-    held, held_gated = hold(after(tokens, a1), gated)
-    b1 = send(z1, FIRST)
-    a3 = send(after(a1, z1, held), SECOND)
+    z1 = send(gated, NEXT_Z)
+    a1 = send(block, FIRST)
+    a2 = send(block, SECOND)
+    z2 = send(block, LAST_Z)
+    held, held_block, biases = hold(tokens, block, input_bias, forget_bias)
+    a3 = send(after(a1, held), SECOND)
+    b1 = send(after(z1, held), FIRST)
     b2 = send(after(z1, a2, z2), SECOND)
-    z3 = send(after(block, a2), FLIP_Z[3])
-    d1 = send(after(z2, b1), FIRST)
+    z3 = send(z2, LAST_Z)
+    d1 = send(after(z2, b1, a3), FIRST)
     b3 = send(after(b1, b2), SECOND)
-    d2 = send(after(z2, a3), SECOND)
-    own_a, part_a = project(columns, (held_gated, a1, a2, a3), held, tokens_other)
-    got_a = send(part_a, OTHER_CORE)
+    d2 = send(after(z2, a3, z3, b2), SECOND)
+    own_a, part_a = project(columns, ((held_block, a1, a2, a3),), held, tokens_other)
     d3 = send(d1, SECOND)
     c1 = send(after(z3, own_a), FIRST)
-    c2 = send(after(z3, own_a), SECOND)
-    own_b, part_b = project(columns, (z1, b1, b2, b3), held, tokens_other)
+    got_a = send(after(part_a, c1), OTHER_CORE)
+    c2 = send(after(z3, b3), SECOND)
+    own_b, part_b = project(columns, ((z1, b1, b2, b3),), held, tokens_other, 0)
     got_b = send(part_b, OTHER_CORE)
-    decay = decay_matrix(own_a, got_a, input_bias, forget_bias)
-    c3 = send(after(c1, own_b, decay), SECOND)
-    own_d, part_d = project(columns, (z2, d1, d2, d3), held, tokens_other)
+    c3 = send(after(c1, own_b), SECOND)
+    decay = decay_matrix(own_b, got_b, biases)
+    own_d, part_d = project(columns, ((z2, d1, d2, d3),), held, tokens_other)
     got_d = send(part_d, OTHER_CORE)
-    own_c, part_c = project(columns, (z3, c1, c2), held, tokens_other)
+    own_c, part_c = project(columns, ((z3, c1, c2),), held, tokens_other)
     got_c = send(part_c, OTHER_CORE)
     c3_other = send(c3, OTHER_CORE)
-    hidden = head(
-        (0, 1, 2, 3), (own_a, own_b, own_d, own_c), (got_a, got_b, got_d, got_c), c3, c3_other, held, decay
-    )
+    assembled, pending = assemble(
+        ((0,), (3,), (1,), (2,)), (own_a, own_b, own_d, own_c), (got_a, got_b, got_d, got_c), c3, held
+    )
+    hidden = head(2, assembled, pending, c3_other, held, decay)
     return (new_master.T, new_first.T, new_second.T, hidden)
 
 

time: 48.8 us -> 47.2 us (0.967)
  waiting for transfers between devices: 14.8 us -> 6.12 us
  starting transfers between devices: 18.1 us -> 24.9 us
    ppermute x21, waiting for transfers between devices: 14.8 us -> 6.12 us  [send(): return lax.ppermute(block, AXES, pairs)]
    ppermute x21, starting transfers between devices: 18.1 us -> 24.9 us  [send(): return lax.ppermute(block, AXES, pairs)]
    pallas_call x7 -> x8, Pallas kernels: 8.24 us -> 8.43 us  [the longest x4 4.8 us: project(): pl.pallas_call(functools.partial(project_kernel, columns, [len(its_blocks...]
    unnamed x6 -> x4, local copies, waits for them, and re-layouts: 2.83 us -> 2.81 us
  transfers between devices with their start and end apart: 21 -> 21, of which waited for: 11 -> 7; matrix products, arithmetic and copies ran while one was open for 0% -> 0% of each run, Pallas kernels for 18% -> 20%
where the time goes in v3:
time: 47.2 us; the launch traced here: 47 us
  starting transfers between devices  24.9 us (53%)
  Pallas kernels  11 us (23%)
  waiting for transfers between devices  6.12 us (13%)
  local copies, waits for them, and re-layouts  2.81 us (6%)
  between operations  2.05 us (4%)
    ppermute x21, starting transfers between devices, send(): return lax.ppermute(block, AXES, pairs)  24.9 us
    ppermute x21, waiting for transfers between devices, send(): return lax.ppermute(block, AXES, pairs)  6.12 us
    pallas_call x4, Pallas kernels, project(): pl.pallas_call(functools.partial(project_kernel, columns, [len(its_blocks...  4.8 us
    unnamed x4, local copies, waits for them, and re-layouts  2.81 us
    pallas_call x1, Pallas kernels, adam_step(): pl.pallas_call(adam_kernel, grid=(steps,), in_specs=[spec] * 4 + [pl.Bloc...  2.6 us
    pallas_call x1, Pallas kernels, head(): pl.pallas_call(functools.partial(head_kernel, offset), in_specs=[VMEM] *...  1.73 us
  transfers between devices with their start and end apart: 21, of which 7 were waited for; matrix products, arithmetic and copies ran while one was open for 0% of the time, Pallas kernels for 20%

profile of v3, /device:TPU:0, one launch (start us, length us, event | category | flops | bytes accessed | tf_op | source)
XLA Modules:
  0.0 47.0 jit_solution(4499543247282965953)
XLA Ops:
  1.1 2.6 %adam.1 = (f32[96,1024]{1,0:T(8,128)}, f32[96,1024]{1,0:T(8,128)}, f32[96,1024]{1,0:T(8,128)}, bf16[96,1024]{1,0:T(8,128)(2,1)}, bf16[112,1024]{1,0:T(8,128)(2,1)}) custom-call(f32[96,1024]{1,0:T(8,128)} %bitcast.12, f32[96,1024]{1,0:T(8,128)} %bitcast.13, f32[96,1024]{1,0:T(8,128)} %bitcast.14, f32[96,1024]{1,0:T(8,128)} %bitcast.15, bf16[2,1024]{1,0:T(2,128)(2,1)} %bitcast.16), custom_call_target="tpu_custom_call" | custom-call | tf_op jit(solution)/shard_map/adam/pallas_call | solution.py:133
  3.8 2.7 %collective-permute-start.4 = (bf16[112,1024]{1,0:T(8,128)(2,1)}, bf16[112,1024]{1,0:T(8,128)(2,1)S(1)}, u32[]{:S(2)}, u32[]{:S(2)}) collective-permute-start(bf16[112,1024]{1,0:T(8,128)(2,1)} %get-tuple-element.40), channel_id=1, source_target_pairs={{0,8},{1,9},{2,10},{3,11},{4,12},{5,13},{6,14},{7,15},{8,16},{9,17... | collective-permute-start | bytes 688136 | tf_op jit(solution)/shard_map/ppermute | solution.py:95
  6.4 1.5 %collective-permute-start.1 = (bf16[96,1024]{1,0:T(8,128)(2,1)}, bf16[96,1024]{1,0:T(8,128)(2,1)S(1)}, u32[]{:S(2)}, u32[]{:S(2)}) collective-permute-start(bf16[96,1024]{1,0:T(8,128)(2,1)} %get-tuple-element.35.gated), channel_id=1, source_target_pairs={{0,4},{1,3},{2,6},{3,1},{4,0},{5,7},{6,2},{7,5},{8,12},{9,11},{10,... | collective-permute-start | bytes 589832 | tf_op jit(solution)/shard_map/ppermute | solution.py:95
  7.9 2.2 %collective-permute-start.6 = (bf16[96,1024]{1,0:T(8,128)(2,1)}, bf16[96,1024]{1,0:T(8,128)(2,1)S(1)}, u32[]{:S(2)}, u32[]{:S(2)}) collective-permute-start(bf16[96,1024]{1,0:T(8,128)(2,1)} %get-tuple-element.35.gated), channel_id=1, source_target_pairs={{0,24},{1,25},{2,26},{3,27},{4,28},{5,29},{6,30},{7,31},{8,0},{9,1... | collective-permute-start | bytes 589832 | tf_op jit(solution)/shard_map/ppermute | solution.py:95
  10.2 1.5 %collective-permute-start = (bf16[96,1024]{1,0:T(8,128)(2,1)}, bf16[96,1024]{1,0:T(8,128)(2,1)S(1)}, u32[]{:S(2)}, u32[]{:S(2)}) collective-permute-start(bf16[96,1024]{1,0:T(8,128)(2,1)} %get-tuple-element.35.gated), channel_id=1, source_target_pairs={{0,2},{1,5},{2,0},{3,7},{4,6},{5,1},{6,4},{7,3},{8,10},{9,13},{10,... | collective-permute-start | bytes 589832 | tf_op jit(solution)/shard_map/ppermute | solution.py:95
  13.0 1.9 %copy-done = bf16[384,4096]{1,0:T(8,128)(2,1)S(1)} copy-done((bf16[384,4096]{1,0:T(8,128)(2,1)S(1)}, bf16[384,4096]{1,0:T(8,128)(2,1)}, u32[]{:S(2)}) %copy-start) | copy-done | bytes 3145752
  14.9 0.9 %copy-done.1 = bf16[96,1024]{1,0:T(8,128)(2,1)S(1)} copy-done((bf16[96,1024]{1,0:T(8,128)(2,1)S(1)}, bf16[96,1024]{1,0:T(8,128)(2,1)}, u32[]{:S(2)}) %copy-start.1) | copy-done | bytes 196632
  17.0 2.1 %collective-permute-done.6.refs_0_ = bf16[96,1024]{1,0:T(8,128)(2,1)S(1)} collective-permute-done((bf16[96,1024]{1,0:T(8,128)(2,1)}, bf16[96,1024]{1,0:T(8,128)(2,1)S(1)}, u32[]{:S(2)}, u32[]{:S(2)}) %collective-permute-start.6) | collective-permute-done | bytes 196640 | tf_op jit(solution)/shard_map/ppermute | solution.py:95
  19.1 1.5 %collective-permute-start.7 = (bf16[112,1024]{1,0:T(8,128)(2,1)S(1)}, bf16[112,1024]{1,0:T(8,128)(2,1)S(1)}, u32[]{:S(2)}, u32[]{:S(2)}) collective-permute-start(bf16[112,1024]{1,0:T(8,128)(2,1)S(1)} %collective-permute-done.4.refs_0_), channel_id=1, source_target_pairs={{0,4},{1,3},{2,6},{3,1},{4,0},{5,7},{6,2},{7,5},{8,12},{9,11},{10,... | collective-permute-start | bytes 688136 | tf_op jit(solution)/shard_map/ppermute | solution.py:95
  21.1 3.2 %collective-permute-start.10 = (bf16[96,1024]{1,0:T(8,128)(2,1)S(1)}, bf16[96,1024]{1,0:T(8,128)(2,1)S(1)}, u32[]{:S(2)}, u32[]{:S(2)}) collective-permute-start(bf16[96,1024]{1,0:T(8,128)(2,1)S(1)} %collective-permute-done.6.refs_0_), channel_id=1, source_target_pairs={{0,24},{1,25},{2,26},{3,27},{4,28},{5,29},{6,30},{7,31},{8,0},{9,1... | collective-permute-start | bytes 589832 | tf_op jit(solution)/shard_map/ppermute | solution.py:95
  24.4 0.7 %collective-permute-done.7.refs_2_ = bf16[112,1024]{1,0:T(8,128)(2,1)S(1)} collective-permute-done((bf16[112,1024]{1,0:T(8,128)(2,1)S(1)}, bf16[112,1024]{1,0:T(8,128)(2,1)S(1)}, u32[]{:S(2)}, u32[]{:S(2)}) %collective-permute-start.7) | collective-permute-done | bytes 229408 | tf_op jit(solution)/shard_map/ppermute | solution.py:95
  25.1 1.5 %collective-permute-start.8 = (bf16[112,1024]{1,0:T(8,128)(2,1)S(1)}, bf16[112,1024]{1,0:T(8,128)(2,1)S(1)}, u32[]{:S(2)}, u32[]{:S(2)}) collective-permute-start(bf16[112,1024]{1,0:T(8,128)(2,1)S(1)} %collective-permute-done.5.refs_1_), channel_id=1, source_target_pairs={{0,4},{1,3},{2,6},{3,1},{4,0},{5,7},{6,2},{7,5},{8,12},{9,11},{10,... | collective-permute-start | bytes 688136 | tf_op jit(solution)/shard_map/ppermute | solution.py:95
  27.2 1.2 %collective-permute-start.9 = (bf16[96,1024]{1,0:T(8,128)(2,1)S(1)}, bf16[96,1024]{1,0:T(8,128)(2,1)S(1)}, u32[]{:S(2)}, u32[]{:S(2)}) collective-permute-start(bf16[96,1024]{1,0:T(8,128)(2,1)S(1)} %collective-permute-done.6.refs_0_), channel_id=1, source_target_pairs={{0,2},{1,5},{2,0},{3,7},{4,6},{5,1},{6,4},{7,3},{8,10},{9,13},{10,... | collective-permute-start | bytes 589832 | tf_op jit(solution)/shard_map/ppermute | solution.py:95
  28.4 1.2 %project.4 = (f32[192,384]{1,0:T(8,128)S(1)}, f32[192,384]{1,0:T(8,128)S(1)}) custom-call(bf16[96,1024]{1,0:T(8,128)(2,1)S(1)} %get-tuple-element.36.refs_0_, bf16[96,1024]{1,0:T(8,128)(2,1)S(1)} %collective-permute-done.refs_1_, bf16[96,1024]{1,0:T(8,128)(2,1)S(1)} %collective-permute-done.1.refs_2_, bf16[96,1024]{1,0:T(8,128)(2,1)S(1)} %collective-permute-done.2.refs_3_, ...), custom_call_target="tpu_custom_call" | custom-call | tf_op jit(solution)/shard_map/project/pallas_call | solution.py:219
  29.6 0.9 %collective-permute-start.13 = (bf16[96,1024]{1,0:T(8,128)(2,1)S(1)}, bf16[96,1024]{1,0:T(8,128)(2,1)S(1)}, u32[]{:S(2)}, u32[]{:S(2)}) collective-permute-start(bf16[96,1024]{1,0:T(8,128)(2,1)S(1)} %collective-permute-done.10.refs_0_), channel_id=1, source_target_pairs={{0,2},{1,5},{2,0},{3,7},{4,6},{5,1},{6,4},{7,3},{8,10},{9,13},{10,... | collective-permute-start | bytes 589832 | tf_op jit(solution)/shard_map/ppermute | solution.py:95
  30.6 1.5 %collective-permute-start.11 = (bf16[96,1024]{1,0:T(8,128)(2,1)S(1)}, bf16[96,1024]{1,0:T(8,128)(2,1)S(1)}, u32[]{:S(2)}, u32[]{:S(2)}) collective-permute-start(bf16[96,1024]{1,0:T(8,128)(2,1)S(1)} %collective-permute-done.6.refs_0_), channel_id=1, source_target_pairs={{0,4},{1,3},{2,6},{3,1},{4,0},{5,7},{6,2},{7,5},{8,12},{9,11},{10,... | collective-permute-start | bytes 589832 | tf_op jit(solution)/shard_map/ppermute | solution.py:95
  32.1 1.2 %collective-permute-done.9.refs_1_ = bf16[96,1024]{1,0:T(8,128)(2,1)S(1)} collective-permute-done((bf16[96,1024]{1,0:T(8,128)(2,1)S(1)}, bf16[96,1024]{1,0:T(8,128)(2,1)S(1)}, u32[]{:S(2)}, u32[]{:S(2)}) %collective-permute-start.9) | collective-permute-done | bytes 196640 | tf_op jit(solution)/shard_map/ppermute | solution.py:95
  33.3 2.2 %collective-permute-start.12 = (bf16[96,1024]{1,0:T(8,128)(2,1)S(1)}, bf16[96,1024]{1,0:T(8,128)(2,1)S(1)}, u32[]{:S(2)}, u32[]{:S(2)}) collective-permute-start(bf16[96,1024]{1,0:T(8,128)(2,1)S(1)} %collective-permute-done.9.refs_1_), channel_id=1, source_target_pairs={{0,4},{1,3},{2,6},{3,1},{4,0},{5,7},{6,2},{7,5},{8,12},{9,11},{10,... | collective-permute-start | bytes 589832 | tf_op jit(solution)/shard_map/ppermute | solution.py:95
  35.5 1.2 %project.5 = (f32[208,384]{1,0:T(8,128)S(1)}, f32[208,384]{1,0:T(8,128)S(1)}) custom-call(bf16[112,1024]{1,0:T(8,128)(2,1)S(1)} %collective-permute-done.4.refs_0_, bf16[112,1024]{1,0:T(8,128)(2,1)S(1)} %collective-permute-done.5.refs_1_, bf16[112,1024]{1,0:T(8,128)(2,1)S(1)} %collective-permute-done.7.refs_2_, ...), custom_call_target="tpu_custom_call" | custom-call | tf_op jit(solution)/shard_map/project/pallas_call | solution.py:219
  37.4 2.2 %collective-permute-start.19 = (bf16[96,1024]{1,0:T(8,128)(2,1)S(1)}, bf16[96,1024]{1,0:T(8,128)(2,1)S(1)}, u32[]{:S(2)}, u32[]{:S(2)}) collective-permute-start(bf16[96,1024]{1,0:T(8,128)(2,1)S(1)} %collective-permute-done.13.refs_1_), channel_id=1, source_target_pairs={{0,4},{1,3},{2,6},{3,1},{4,0},{5,7},{6,2},{7,5},{8,12},{9,11},{10,... | collective-permute-start | bytes 589832 | tf_op jit(solution)/shard_map/ppermute | solution.py:95
  39.7 1.2 %project.6 = (f32[192,384]{1,0:T(8,128)S(1)}, f32[192,384]{1,0:T(8,128)S(1)}) custom-call(bf16[96,1024]{1,0:T(8,128)(2,1)S(1)} %collective-permute-done.6.refs_0_, bf16[96,1024]{1,0:T(8,128)(2,1)S(1)} %collective-permute-done.9.refs_1_, bf16[96,1024]{1,0:T(8,128)(2,1)S(1)} %collective-permute-done.11.refs_2_, ...), custom_call_target="tpu_custom_call" | custom-call | tf_op jit(solution)/shard_map/project/pallas_call | solution.py:219
  41.7 1.2 %project.7 = (f32[192,384]{1,0:T(8,128)S(1)}, f32[192,384]{1,0:T(8,128)S(1)}) custom-call(bf16[96,1024]{1,0:T(8,128)(2,1)S(1)} %collective-permute-done.10.refs_0_, bf16[96,1024]{1,0:T(8,128)(2,1)S(1)} %collective-permute-done.13.refs_1_, bf16[96,1024]{1,0:T(8,128)(2,1)S(1)} %collective-permute-done.14.refs_2_, ...), custom_call_target="tpu_custom_call" | custom-call | tf_op jit(solution)/shard_map/project/pallas_call | solution.py:219
  43.8 0.9 %decay.1 = f32[384,384]{1,0:T(8,128)S(1)} custom-call(f32[208,384]{1,0:T(8,128)S(1)} %get-tuple-element.44.refs_1_.own, f32[208,384]{1,0:T(8,128)S(1)} %collective-permute-done.16.refs_5_.got, f32[2,8,384]{2,1,0:T(8,128)S(1)} %get-tuple-element.59.biases), custom_call_target="tpu_custom_call" | custom-call | tf_op jit(solution)/shard_map/decay/pallas_call | solution.py:249
  45.2 1.7 %head.1 = bf16[384,256]{1,0:T(8,128)(2,1)} custom-call(bf16[768,384]{1,0:T(8,128)(2,1)S(1)} %get-tuple-element.57.assembled, f32[96,384]{1,0:T(8,128)S(1)} %get-tuple-element.58.pending, bf16[96,1024]{1,0:T(8,128)(2,1)S(1)} %collective-permute-done.20.last_other, bf16[384,4096]{1,0:T(8,128)(2,1)S(1)} %get-tuple-element.37.refs_4_.refs_3_.refs_9_.tokens, ...), custom_call_target="tpu_custom_call" | custom-call | tf_op jit(solution)/shard_map/head/pallas_call | solution.py:314
  (31 shorter events, 5.8 us)
Async XLA Ops:
  0.6 27.8 %collective-permute-start.3 = (bf16[384,4096]{1,0:T(8,128)(2,1)}, bf16[384,4096]{1,0:T(8,128)(2,1)S(1)}, u32[]{:S(2)}, u32[]{:S(2)}) collective-permute-start(bf16[384,4096]{1,0:T(8,128)(2,1)} %tokens.1), channel_id=1, source_target_pairs={{0,1},{1,0},{2,3},{3,2},{4,5},{5,4},{6,7},{7,6},{8,9},{9,8},{10,11... | collective-permute-start | bytes 9437192 | tf_op jit(solution)/shard_map/ppermute | solution.py:95
  3.8 12.6 %collective-permute-start.4 = (bf16[112,1024]{1,0:T(8,128)(2,1)}, bf16[112,1024]{1,0:T(8,128)(2,1)S(1)}, u32[]{:S(2)}, u32[]{:S(2)}) collective-permute-start(bf16[112,1024]{1,0:T(8,128)(2,1)} %get-tuple-element.40), channel_id=1, source_target_pairs={{0,8},{1,9},{2,10},{3,11},{4,12},{5,13},{6,14},{7,15},{8,16},{9,17... | collective-permute-start | bytes 688136 | tf_op jit(solution)/shard_map/ppermute | solution.py:95
  6.4 10.5 %collective-permute-start.1 = (bf16[96,1024]{1,0:T(8,128)(2,1)}, bf16[96,1024]{1,0:T(8,128)(2,1)S(1)}, u32[]{:S(2)}, u32[]{:S(2)}) collective-permute-start(bf16[96,1024]{1,0:T(8,128)(2,1)} %get-tuple-element.35.gated), channel_id=1, source_target_pairs={{0,4},{1,3},{2,6},{3,1},{4,0},{5,7},{6,2},{7,5},{8,12},{9,11},{10,... | collective-permute-start | bytes 589832 | tf_op jit(solution)/shard_map/ppermute | solution.py:95
  7.9 11.2 %collective-permute-start.6 = (bf16[96,1024]{1,0:T(8,128)(2,1)}, bf16[96,1024]{1,0:T(8,128)(2,1)S(1)}, u32[]{:S(2)}, u32[]{:S(2)}) collective-permute-start(bf16[96,1024]{1,0:T(8,128)(2,1)} %get-tuple-element.35.gated), channel_id=1, source_target_pairs={{0,24},{1,25},{2,26},{3,27},{4,28},{5,29},{6,30},{7,31},{8,0},{9,1... | collective-permute-start | bytes 589832 | tf_op jit(solution)/shard_map/ppermute | solution.py:95
  10.2 10.4 %collective-permute-start = (bf16[96,1024]{1,0:T(8,128)(2,1)}, bf16[96,1024]{1,0:T(8,128)(2,1)S(1)}, u32[]{:S(2)}, u32[]{:S(2)}) collective-permute-start(bf16[96,1024]{1,0:T(8,128)(2,1)} %get-tuple-element.35.gated), channel_id=1, source_target_pairs={{0,2},{1,5},{2,0},{3,7},{4,6},{5,1},{6,4},{7,3},{8,10},{9,13},{10,... | collective-permute-start | bytes 589832 | tf_op jit(solution)/shard_map/ppermute | solution.py:95
  13.0 1.9 %copy-start = (bf16[384,4096]{1,0:T(8,128)(2,1)S(1)}, bf16[384,4096]{1,0:T(8,128)(2,1)}, u32[]{:S(2)}) copy-start(bf16[384,4096]{1,0:T(8,128)(2,1)} %tokens.1) | copy-start | bytes 9437188
  14.9 0.9 %copy-start.1 = (bf16[96,1024]{1,0:T(8,128)(2,1)S(1)}, bf16[96,1024]{1,0:T(8,128)(2,1)}, u32[]{:S(2)}) copy-start(bf16[96,1024]{1,0:T(8,128)(2,1)} %get-tuple-element.35.gated) | copy-start | bytes 589828
  16.4 8.0 %collective-permute-start.5 = (bf16[112,1024]{1,0:T(8,128)(2,1)S(1)}, bf16[112,1024]{1,0:T(8,128)(2,1)S(1)}, u32[]{:S(2)}, u32[]{:S(2)}) collective-permute-start(bf16[112,1024]{1,0:T(8,128)(2,1)S(1)} %collective-permute-done.4.refs_0_), channel_id=1, source_target_pairs={{0,2},{1,5},{2,0},{3,7},{4,6},{5,1},{6,4},{7,3},{8,10},{9,13},{10,... | collective-permute-start | bytes 688136 | tf_op jit(solution)/shard_map/ppermute | solution.py:95
  19.1 6.0 %collective-permute-start.7 = (bf16[112,1024]{1,0:T(8,128)(2,1)S(1)}, bf16[112,1024]{1,0:T(8,128)(2,1)S(1)}, u32[]{:S(2)}, u32[]{:S(2)}) collective-permute-start(bf16[112,1024]{1,0:T(8,128)(2,1)S(1)} %collective-permute-done.4.refs_0_), channel_id=1, source_target_pairs={{0,4},{1,3},{2,6},{3,1},{4,0},{5,7},{6,2},{7,5},{8,12},{9,11},{10,... | collective-permute-start | bytes 688136 | tf_op jit(solution)/shard_map/ppermute | solution.py:95
  20.6 6.6 %collective-permute-start.2 = (bf16[96,1024]{1,0:T(8,128)(2,1)S(1)}, bf16[96,1024]{1,0:T(8,128)(2,1)S(1)}, u32[]{:S(2)}, u32[]{:S(2)}) collective-permute-start(bf16[96,1024]{1,0:T(8,128)(2,1)S(1)} %collective-permute-done.refs_1_), channel_id=1, source_target_pairs={{0,4},{1,3},{2,6},{3,1},{4,0},{5,7},{6,2},{7,5},{8,12},{9,11},{10,... | collective-permute-start | bytes 589832 | tf_op jit(solution)/shard_map/ppermute | solution.py:95
  21.1 8.5 %collective-permute-start.10 = (bf16[96,1024]{1,0:T(8,128)(2,1)S(1)}, bf16[96,1024]{1,0:T(8,128)(2,1)S(1)}, u32[]{:S(2)}, u32[]{:S(2)}) collective-permute-start(bf16[96,1024]{1,0:T(8,128)(2,1)S(1)} %collective-permute-done.6.refs_0_), channel_id=1, source_target_pairs={{0,24},{1,25},{2,26},{3,27},{4,28},{5,29},{6,30},{7,31},{8,0},{9,1... | collective-permute-start | bytes 589832 | tf_op jit(solution)/shard_map/ppermute | solution.py:95
  25.1 10.3 %collective-permute-start.8 = (bf16[112,1024]{1,0:T(8,128)(2,1)S(1)}, bf16[112,1024]{1,0:T(8,128)(2,1)S(1)}, u32[]{:S(2)}, u32[]{:S(2)}) collective-permute-start(bf16[112,1024]{1,0:T(8,128)(2,1)S(1)} %collective-permute-done.5.refs_1_), channel_id=1, source_target_pairs={{0,4},{1,3},{2,6},{3,1},{4,0},{5,7},{6,2},{7,5},{8,12},{9,11},{10,... | collective-permute-start | bytes 688136 | tf_op jit(solution)/shard_map/ppermute | solution.py:95
  27.2 6.0 %collective-permute-start.9 = (bf16[96,1024]{1,0:T(8,128)(2,1)S(1)}, bf16[96,1024]{1,0:T(8,128)(2,1)S(1)}, u32[]{:S(2)}, u32[]{:S(2)}) collective-permute-start(bf16[96,1024]{1,0:T(8,128)(2,1)S(1)} %collective-permute-done.6.refs_0_), channel_id=1, source_target_pairs={{0,2},{1,5},{2,0},{3,7},{4,6},{5,1},{6,4},{7,3},{8,10},{9,13},{10,... | collective-permute-start | bytes 589832 | tf_op jit(solution)/shard_map/ppermute | solution.py:95
  29.6 7.8 %collective-permute-start.13 = (bf16[96,1024]{1,0:T(8,128)(2,1)S(1)}, bf16[96,1024]{1,0:T(8,128)(2,1)S(1)}, u32[]{:S(2)}, u32[]{:S(2)}) collective-permute-start(bf16[96,1024]{1,0:T(8,128)(2,1)S(1)} %collective-permute-done.10.refs_0_), channel_id=1, source_target_pairs={{0,2},{1,5},{2,0},{3,7},{4,6},{5,1},{6,4},{7,3},{8,10},{9,13},{10,... | collective-permute-start | bytes 589832 | tf_op jit(solution)/shard_map/ppermute | solution.py:95
  30.6 9.1 %collective-permute-start.11 = (bf16[96,1024]{1,0:T(8,128)(2,1)S(1)}, bf16[96,1024]{1,0:T(8,128)(2,1)S(1)}, u32[]{:S(2)}, u32[]{:S(2)}) collective-permute-start(bf16[96,1024]{1,0:T(8,128)(2,1)S(1)} %collective-permute-done.6.refs_0_), channel_id=1, source_target_pairs={{0,4},{1,3},{2,6},{3,1},{4,0},{5,7},{6,2},{7,5},{8,12},{9,11},{10,... | collective-permute-start | bytes 589832 | tf_op jit(solution)/shard_map/ppermute | solution.py:95
  33.3 6.4 %collective-permute-start.12 = (bf16[96,1024]{1,0:T(8,128)(2,1)S(1)}, bf16[96,1024]{1,0:T(8,128)(2,1)S(1)}, u32[]{:S(2)}, u32[]{:S(2)}) collective-permute-start(bf16[96,1024]{1,0:T(8,128)(2,1)S(1)} %collective-permute-done.9.refs_1_), channel_id=1, source_target_pairs={{0,4},{1,3},{2,6},{3,1},{4,0},{5,7},{6,2},{7,5},{8,12},{9,11},{10,... | collective-permute-start | bytes 589832 | tf_op jit(solution)/shard_map/ppermute | solution.py:95
  35.5 6.2 %collective-permute-start.14 = (bf16[96,1024]{1,0:T(8,128)(2,1)S(1)}, bf16[96,1024]{1,0:T(8,128)(2,1)S(1)}, u32[]{:S(2)}, u32[]{:S(2)}) collective-permute-start(bf16[96,1024]{1,0:T(8,128)(2,1)S(1)} %collective-permute-done.10.refs_0_), channel_id=1, source_target_pairs={{0,4},{1,3},{2,6},{3,1},{4,0},{5,7},{6,2},{7,5},{8,12},{9,11},{10,... | collective-permute-start | bytes 589832 | tf_op jit(solution)/shard_map/ppermute | solution.py:95
  37.4 6.3 %collective-permute-start.19 = (bf16[96,1024]{1,0:T(8,128)(2,1)S(1)}, bf16[96,1024]{1,0:T(8,128)(2,1)S(1)}, u32[]{:S(2)}, u32[]{:S(2)}) collective-permute-start(bf16[96,1024]{1,0:T(8,128)(2,1)S(1)} %collective-permute-done.13.refs_1_), channel_id=1, source_target_pairs={{0,4},{1,3},{2,6},{3,1},{4,0},{5,7},{6,2},{7,5},{8,12},{9,11},{10,... | collective-permute-start | bytes 589832 | tf_op jit(solution)/shard_map/ppermute | solution.py:95
  39.7 4.1 %collective-permute-start.16 = (f32[208,384]{1,0:T(8,128)S(1)}, f32[208,384]{1,0:T(8,128)S(1)}, u32[]{:S(2)}, u32[]{:S(2)}) collective-permute-start(f32[208,384]{1,0:T(8,128)S(1)} %get-tuple-element.53), channel_id=1, source_target_pairs={{0,1},{1,0},{2,3},{3,2},{4,5},{5,4},{6,7},{7,6},{8,9},{9,8},{10,11... | collective-permute-start | bytes 958472 | tf_op jit(solution)/shard_map/ppermute | solution.py:95
  40.9 3.8 %collective-permute-start.17 = (f32[192,384]{1,0:T(8,128)S(1)}, f32[192,384]{1,0:T(8,128)S(1)}, u32[]{:S(2)}, u32[]{:S(2)}) collective-permute-start(f32[192,384]{1,0:T(8,128)S(1)} %get-tuple-element.54), channel_id=1, source_target_pairs={{0,1},{1,0},{2,3},{3,2},{4,5},{5,4},{6,7},{7,6},{8,9},{9,8},{10,11... | collective-permute-start | bytes 884744 | tf_op jit(solution)/shard_map/ppermute | solution.py:95
  41.5 3.2 %collective-permute-start.15 = (f32[192,384]{1,0:T(8,128)S(1)}, f32[192,384]{1,0:T(8,128)S(1)}, u32[]{:S(2)}, u32[]{:S(2)}) collective-permute-start(f32[192,384]{1,0:T(8,128)S(1)} %get-tuple-element.52), channel_id=1, source_target_pairs={{0,1},{1,0},{2,3},{3,2},{4,5},{5,4},{6,7},{7,6},{8,9},{9,8},{10,11... | collective-permute-start | bytes 884744 | tf_op jit(solution)/shard_map/ppermute | solution.py:95
  42.9 1.8 %collective-permute-start.18 = (f32[192,384]{1,0:T(8,128)S(1)}, f32[192,384]{1,0:T(8,128)S(1)}, u32[]{:S(2)}, u32[]{:S(2)}) collective-permute-start(f32[192,384]{1,0:T(8,128)S(1)} %get-tuple-element.55), channel_id=1, source_target_pairs={{0,1},{1,0},{2,3},{3,2},{4,5},{5,4},{6,7},{7,6},{8,9},{9,8},{10,11... | collective-permute-start | bytes 884744 | tf_op jit(solution)/shard_map/ppermute | solution.py:95
  43.8 1.4 %collective-permute-start.20 = (bf16[96,1024]{1,0:T(8,128)(2,1)S(1)}, bf16[96,1024]{1,0:T(8,128)(2,1)S(1)}, u32[]{:S(2)}, u32[]{:S(2)}) collective-permute-start(bf16[96,1024]{1,0:T(8,128)(2,1)S(1)} %collective-permute-done.19.refs_8_), channel_id=1, source_target_pairs={{0,1},{1,0},{2,3},{3,2},{4,5},{5,4},{6,7},{7,6},{8,9},{9,8},{10,11... | collective-permute-start | bytes 589832 | tf_op jit(solution)/shard_map/ppermute | solution.py:95

commit v4 on v3

--- a/solution.py
+++ b/solution.py
@@ -306,7 +306,7 @@
     weighted = scores * decay[...]
     normalizer = jnp.sum(weighted, axis=0, keepdims=True)
     numerator = jnp.dot(value, weighted.astype(jnp.bfloat16), preferred_element_type=jnp.float32)
-    out[...] = (numerator / jnp.maximum(jnp.abs(normalizer), 1.0)).T.astype(jnp.bfloat16)
+    out[...] = (numerator / jnp.maximum(jnp.abs(normalizer), 1.0)).astype(jnp.bfloat16).T
 
 
 def head(offset, assembled, pending, last_other, tokens, decay):

time: 47.2 us -> 47.2 us (level)
  no operation moved by 1% of the time
where the time goes in v4:
time: 47.2 us; the launch traced here: 46.9 us
  starting transfers between devices  24.9 us (53%)
  Pallas kernels  11 us (23%)
  waiting for transfers between devices  6.12 us (13%)
  local copies, waits for them, and re-layouts  2.81 us (6%)
  between operations  2.05 us (4%)
    ppermute x21, starting transfers between devices, send(): return lax.ppermute(block, AXES, pairs)  24.9 us
    ppermute x21, waiting for transfers between devices, send(): return lax.ppermute(block, AXES, pairs)  6.12 us
    pallas_call x4, Pallas kernels, project(): pl.pallas_call(functools.partial(project_kernel, columns, [len(its_blocks...  4.8 us
    unnamed x4, local copies, waits for them, and re-layouts  2.81 us
    pallas_call x1, Pallas kernels, adam_step(): pl.pallas_call(adam_kernel, grid=(steps,), in_specs=[spec] * 4 + [pl.Bloc...  2.6 us
    pallas_call x1, Pallas kernels, head(): pl.pallas_call(functools.partial(head_kernel, offset), in_specs=[VMEM] *...  1.7 us
  transfers between devices with their start and end apart: 21, of which 7 were waited for; matrix products, arithmetic and copies ran while one was open for 0% of the time, Pallas kernels for 20%

profile of v4, /device:TPU:0, one launch (start us, length us, event | category | flops | bytes accessed | tf_op | source)
XLA Modules:
  0.0 46.9 jit_solution(597870685046107911)
XLA Ops:
  1.1 2.6 %adam.1 = (f32[96,1024]{1,0:T(8,128)}, f32[96,1024]{1,0:T(8,128)}, f32[96,1024]{1,0:T(8,128)}, bf16[96,1024]{1,0:T(8,128)(2,1)}, bf16[112,1024]{1,0:T(8,128)(2,1)}) custom-call(f32[96,1024]{1,0:T(8,128)} %bitcast.12, f32[96,1024]{1,0:T(8,128)} %bitcast.13, f32[96,1024]{1,0:T(8,128)} %bitcast.14, f32[96,1024]{1,0:T(8,128)} %bitcast.15, bf16[2,1024]{1,0:T(2,128)(2,1)} %bitcast.16), custom_call_target="tpu_custom_call" | custom-call | tf_op jit(solution)/shard_map/adam/pallas_call | solution.py:133
  3.8 2.7 %collective-permute-start.4 = (bf16[112,1024]{1,0:T(8,128)(2,1)}, bf16[112,1024]{1,0:T(8,128)(2,1)S(1)}, u32[]{:S(2)}, u32[]{:S(2)}) collective-permute-start(bf16[112,1024]{1,0:T(8,128)(2,1)} %get-tuple-element.40), channel_id=1, source_target_pairs={{0,8},{1,9},{2,10},{3,11},{4,12},{5,13},{6,14},{7,15},{8,16},{9,17... | collective-permute-start | bytes 688136 | tf_op jit(solution)/shard_map/ppermute | solution.py:95
  6.4 1.5 %collective-permute-start.1 = (bf16[96,1024]{1,0:T(8,128)(2,1)}, bf16[96,1024]{1,0:T(8,128)(2,1)S(1)}, u32[]{:S(2)}, u32[]{:S(2)}) collective-permute-start(bf16[96,1024]{1,0:T(8,128)(2,1)} %get-tuple-element.35.gated), channel_id=1, source_target_pairs={{0,4},{1,3},{2,6},{3,1},{4,0},{5,7},{6,2},{7,5},{8,12},{9,11},{10,... | collective-permute-start | bytes 589832 | tf_op jit(solution)/shard_map/ppermute | solution.py:95
  7.9 2.2 %collective-permute-start.6 = (bf16[96,1024]{1,0:T(8,128)(2,1)}, bf16[96,1024]{1,0:T(8,128)(2,1)S(1)}, u32[]{:S(2)}, u32[]{:S(2)}) collective-permute-start(bf16[96,1024]{1,0:T(8,128)(2,1)} %get-tuple-element.35.gated), channel_id=1, source_target_pairs={{0,24},{1,25},{2,26},{3,27},{4,28},{5,29},{6,30},{7,31},{8,0},{9,1... | collective-permute-start | bytes 589832 | tf_op jit(solution)/shard_map/ppermute | solution.py:95
  10.2 1.5 %collective-permute-start = (bf16[96,1024]{1,0:T(8,128)(2,1)}, bf16[96,1024]{1,0:T(8,128)(2,1)S(1)}, u32[]{:S(2)}, u32[]{:S(2)}) collective-permute-start(bf16[96,1024]{1,0:T(8,128)(2,1)} %get-tuple-element.35.gated), channel_id=1, source_target_pairs={{0,2},{1,5},{2,0},{3,7},{4,6},{5,1},{6,4},{7,3},{8,10},{9,13},{10,... | collective-permute-start | bytes 589832 | tf_op jit(solution)/shard_map/ppermute | solution.py:95
  13.0 1.9 %copy-done = bf16[384,4096]{1,0:T(8,128)(2,1)S(1)} copy-done((bf16[384,4096]{1,0:T(8,128)(2,1)S(1)}, bf16[384,4096]{1,0:T(8,128)(2,1)}, u32[]{:S(2)}) %copy-start) | copy-done | bytes 3145752
  14.9 0.9 %copy-done.1 = bf16[96,1024]{1,0:T(8,128)(2,1)S(1)} copy-done((bf16[96,1024]{1,0:T(8,128)(2,1)S(1)}, bf16[96,1024]{1,0:T(8,128)(2,1)}, u32[]{:S(2)}) %copy-start.1) | copy-done | bytes 196632
  17.0 2.1 %collective-permute-done.6.refs_0_ = bf16[96,1024]{1,0:T(8,128)(2,1)S(1)} collective-permute-done((bf16[96,1024]{1,0:T(8,128)(2,1)}, bf16[96,1024]{1,0:T(8,128)(2,1)S(1)}, u32[]{:S(2)}, u32[]{:S(2)}) %collective-permute-start.6) | collective-permute-done | bytes 196640 | tf_op jit(solution)/shard_map/ppermute | solution.py:95
  19.1 1.5 %collective-permute-start.7 = (bf16[112,1024]{1,0:T(8,128)(2,1)S(1)}, bf16[112,1024]{1,0:T(8,128)(2,1)S(1)}, u32[]{:S(2)}, u32[]{:S(2)}) collective-permute-start(bf16[112,1024]{1,0:T(8,128)(2,1)S(1)} %collective-permute-done.4.refs_0_), channel_id=1, source_target_pairs={{0,4},{1,3},{2,6},{3,1},{4,0},{5,7},{6,2},{7,5},{8,12},{9,11},{10,... | collective-permute-start | bytes 688136 | tf_op jit(solution)/shard_map/ppermute | solution.py:95
  21.1 3.2 %collective-permute-start.10 = (bf16[96,1024]{1,0:T(8,128)(2,1)S(1)}, bf16[96,1024]{1,0:T(8,128)(2,1)S(1)}, u32[]{:S(2)}, u32[]{:S(2)}) collective-permute-start(bf16[96,1024]{1,0:T(8,128)(2,1)S(1)} %collective-permute-done.6.refs_0_), channel_id=1, source_target_pairs={{0,24},{1,25},{2,26},{3,27},{4,28},{5,29},{6,30},{7,31},{8,0},{9,1... | collective-permute-start | bytes 589832 | tf_op jit(solution)/shard_map/ppermute | solution.py:95
  24.4 0.7 %collective-permute-done.7.refs_2_ = bf16[112,1024]{1,0:T(8,128)(2,1)S(1)} collective-permute-done((bf16[112,1024]{1,0:T(8,128)(2,1)S(1)}, bf16[112,1024]{1,0:T(8,128)(2,1)S(1)}, u32[]{:S(2)}, u32[]{:S(2)}) %collective-permute-start.7) | collective-permute-done | bytes 229408 | tf_op jit(solution)/shard_map/ppermute | solution.py:95
  25.1 1.5 %collective-permute-start.8 = (bf16[112,1024]{1,0:T(8,128)(2,1)S(1)}, bf16[112,1024]{1,0:T(8,128)(2,1)S(1)}, u32[]{:S(2)}, u32[]{:S(2)}) collective-permute-start(bf16[112,1024]{1,0:T(8,128)(2,1)S(1)} %collective-permute-done.5.refs_1_), channel_id=1, source_target_pairs={{0,4},{1,3},{2,6},{3,1},{4,0},{5,7},{6,2},{7,5},{8,12},{9,11},{10,... | collective-permute-start | bytes 688136 | tf_op jit(solution)/shard_map/ppermute | solution.py:95
  27.2 1.2 %collective-permute-start.9 = (bf16[96,1024]{1,0:T(8,128)(2,1)S(1)}, bf16[96,1024]{1,0:T(8,128)(2,1)S(1)}, u32[]{:S(2)}, u32[]{:S(2)}) collective-permute-start(bf16[96,1024]{1,0:T(8,128)(2,1)S(1)} %collective-permute-done.6.refs_0_), channel_id=1, source_target_pairs={{0,2},{1,5},{2,0},{3,7},{4,6},{5,1},{6,4},{7,3},{8,10},{9,13},{10,... | collective-permute-start | bytes 589832 | tf_op jit(solution)/shard_map/ppermute | solution.py:95
  28.4 1.2 %project.4 = (f32[192,384]{1,0:T(8,128)S(1)}, f32[192,384]{1,0:T(8,128)S(1)}) custom-call(bf16[96,1024]{1,0:T(8,128)(2,1)S(1)} %get-tuple-element.36.refs_0_, bf16[96,1024]{1,0:T(8,128)(2,1)S(1)} %collective-permute-done.refs_1_, bf16[96,1024]{1,0:T(8,128)(2,1)S(1)} %collective-permute-done.1.refs_2_, bf16[96,1024]{1,0:T(8,128)(2,1)S(1)} %collective-permute-done.2.refs_3_, ...), custom_call_target="tpu_custom_call" | custom-call | tf_op jit(solution)/shard_map/project/pallas_call | solution.py:219
  29.6 0.9 %collective-permute-start.13 = (bf16[96,1024]{1,0:T(8,128)(2,1)S(1)}, bf16[96,1024]{1,0:T(8,128)(2,1)S(1)}, u32[]{:S(2)}, u32[]{:S(2)}) collective-permute-start(bf16[96,1024]{1,0:T(8,128)(2,1)S(1)} %collective-permute-done.10.refs_0_), channel_id=1, source_target_pairs={{0,2},{1,5},{2,0},{3,7},{4,6},{5,1},{6,4},{7,3},{8,10},{9,13},{10,... | collective-permute-start | bytes 589832 | tf_op jit(solution)/shard_map/ppermute | solution.py:95
  30.6 1.5 %collective-permute-start.11 = (bf16[96,1024]{1,0:T(8,128)(2,1)S(1)}, bf16[96,1024]{1,0:T(8,128)(2,1)S(1)}, u32[]{:S(2)}, u32[]{:S(2)}) collective-permute-start(bf16[96,1024]{1,0:T(8,128)(2,1)S(1)} %collective-permute-done.6.refs_0_), channel_id=1, source_target_pairs={{0,4},{1,3},{2,6},{3,1},{4,0},{5,7},{6,2},{7,5},{8,12},{9,11},{10,... | collective-permute-start | bytes 589832 | tf_op jit(solution)/shard_map/ppermute | solution.py:95
  32.1 1.2 %collective-permute-done.9.refs_1_ = bf16[96,1024]{1,0:T(8,128)(2,1)S(1)} collective-permute-done((bf16[96,1024]{1,0:T(8,128)(2,1)S(1)}, bf16[96,1024]{1,0:T(8,128)(2,1)S(1)}, u32[]{:S(2)}, u32[]{:S(2)}) %collective-permute-start.9) | collective-permute-done | bytes 196640 | tf_op jit(solution)/shard_map/ppermute | solution.py:95
  33.3 2.2 %collective-permute-start.12 = (bf16[96,1024]{1,0:T(8,128)(2,1)S(1)}, bf16[96,1024]{1,0:T(8,128)(2,1)S(1)}, u32[]{:S(2)}, u32[]{:S(2)}) collective-permute-start(bf16[96,1024]{1,0:T(8,128)(2,1)S(1)} %collective-permute-done.9.refs_1_), channel_id=1, source_target_pairs={{0,4},{1,3},{2,6},{3,1},{4,0},{5,7},{6,2},{7,5},{8,12},{9,11},{10,... | collective-permute-start | bytes 589832 | tf_op jit(solution)/shard_map/ppermute | solution.py:95
  35.5 1.2 %project.5 = (f32[208,384]{1,0:T(8,128)S(1)}, f32[208,384]{1,0:T(8,128)S(1)}) custom-call(bf16[112,1024]{1,0:T(8,128)(2,1)S(1)} %collective-permute-done.4.refs_0_, bf16[112,1024]{1,0:T(8,128)(2,1)S(1)} %collective-permute-done.5.refs_1_, bf16[112,1024]{1,0:T(8,128)(2,1)S(1)} %collective-permute-done.7.refs_2_, ...), custom_call_target="tpu_custom_call" | custom-call | tf_op jit(solution)/shard_map/project/pallas_call | solution.py:219
  37.4 2.2 %collective-permute-start.19 = (bf16[96,1024]{1,0:T(8,128)(2,1)S(1)}, bf16[96,1024]{1,0:T(8,128)(2,1)S(1)}, u32[]{:S(2)}, u32[]{:S(2)}) collective-permute-start(bf16[96,1024]{1,0:T(8,128)(2,1)S(1)} %collective-permute-done.13.refs_1_), channel_id=1, source_target_pairs={{0,4},{1,3},{2,6},{3,1},{4,0},{5,7},{6,2},{7,5},{8,12},{9,11},{10,... | collective-permute-start | bytes 589832 | tf_op jit(solution)/shard_map/ppermute | solution.py:95
  39.7 1.2 %project.6 = (f32[192,384]{1,0:T(8,128)S(1)}, f32[192,384]{1,0:T(8,128)S(1)}) custom-call(bf16[96,1024]{1,0:T(8,128)(2,1)S(1)} %collective-permute-done.6.refs_0_, bf16[96,1024]{1,0:T(8,128)(2,1)S(1)} %collective-permute-done.9.refs_1_, bf16[96,1024]{1,0:T(8,128)(2,1)S(1)} %collective-permute-done.11.refs_2_, ...), custom_call_target="tpu_custom_call" | custom-call | tf_op jit(solution)/shard_map/project/pallas_call | solution.py:219
  41.7 1.2 %project.7 = (f32[192,384]{1,0:T(8,128)S(1)}, f32[192,384]{1,0:T(8,128)S(1)}) custom-call(bf16[96,1024]{1,0:T(8,128)(2,1)S(1)} %collective-permute-done.10.refs_0_, bf16[96,1024]{1,0:T(8,128)(2,1)S(1)} %collective-permute-done.13.refs_1_, bf16[96,1024]{1,0:T(8,128)(2,1)S(1)} %collective-permute-done.14.refs_2_, ...), custom_call_target="tpu_custom_call" | custom-call | tf_op jit(solution)/shard_map/project/pallas_call | solution.py:219
  43.8 0.9 %decay.1 = f32[384,384]{1,0:T(8,128)S(1)} custom-call(f32[208,384]{1,0:T(8,128)S(1)} %get-tuple-element.44.refs_1_.own, f32[208,384]{1,0:T(8,128)S(1)} %collective-permute-done.16.refs_5_.got, f32[2,8,384]{2,1,0:T(8,128)S(1)} %get-tuple-element.59.biases), custom_call_target="tpu_custom_call" | custom-call | tf_op jit(solution)/shard_map/decay/pallas_call | solution.py:249
  45.2 1.7 %head.1 = bf16[384,256]{1,0:T(8,128)(2,1)} custom-call(bf16[768,384]{1,0:T(8,128)(2,1)S(1)} %get-tuple-element.57.assembled, f32[96,384]{1,0:T(8,128)S(1)} %get-tuple-element.58.pending, bf16[96,1024]{1,0:T(8,128)(2,1)S(1)} %collective-permute-done.20.last_other, bf16[384,4096]{1,0:T(8,128)(2,1)S(1)} %get-tuple-element.37.refs_4_.refs_3_.refs_9_.tokens, ...), custom_call_target="tpu_custom_call" | custom-call | tf_op jit(solution)/shard_map/head/pallas_call | solution.py:314
  (31 shorter events, 5.8 us)
Async XLA Ops:
  0.6 27.8 %collective-permute-start.3 = (bf16[384,4096]{1,0:T(8,128)(2,1)}, bf16[384,4096]{1,0:T(8,128)(2,1)S(1)}, u32[]{:S(2)}, u32[]{:S(2)}) collective-permute-start(bf16[384,4096]{1,0:T(8,128)(2,1)} %tokens.1), channel_id=1, source_target_pairs={{0,1},{1,0},{2,3},{3,2},{4,5},{5,4},{6,7},{7,6},{8,9},{9,8},{10,11... | collective-permute-start | bytes 9437192 | tf_op jit(solution)/shard_map/ppermute | solution.py:95
  3.8 12.6 %collective-permute-start.4 = (bf16[112,1024]{1,0:T(8,128)(2,1)}, bf16[112,1024]{1,0:T(8,128)(2,1)S(1)}, u32[]{:S(2)}, u32[]{:S(2)}) collective-permute-start(bf16[112,1024]{1,0:T(8,128)(2,1)} %get-tuple-element.40), channel_id=1, source_target_pairs={{0,8},{1,9},{2,10},{3,11},{4,12},{5,13},{6,14},{7,15},{8,16},{9,17... | collective-permute-start | bytes 688136 | tf_op jit(solution)/shard_map/ppermute | solution.py:95
  6.4 10.5 %collective-permute-start.1 = (bf16[96,1024]{1,0:T(8,128)(2,1)}, bf16[96,1024]{1,0:T(8,128)(2,1)S(1)}, u32[]{:S(2)}, u32[]{:S(2)}) collective-permute-start(bf16[96,1024]{1,0:T(8,128)(2,1)} %get-tuple-element.35.gated), channel_id=1, source_target_pairs={{0,4},{1,3},{2,6},{3,1},{4,0},{5,7},{6,2},{7,5},{8,12},{9,11},{10,... | collective-permute-start | bytes 589832 | tf_op jit(solution)/shard_map/ppermute | solution.py:95
  7.9 11.2 %collective-permute-start.6 = (bf16[96,1024]{1,0:T(8,128)(2,1)}, bf16[96,1024]{1,0:T(8,128)(2,1)S(1)}, u32[]{:S(2)}, u32[]{:S(2)}) collective-permute-start(bf16[96,1024]{1,0:T(8,128)(2,1)} %get-tuple-element.35.gated), channel_id=1, source_target_pairs={{0,24},{1,25},{2,26},{3,27},{4,28},{5,29},{6,30},{7,31},{8,0},{9,1... | collective-permute-start | bytes 589832 | tf_op jit(solution)/shard_map/ppermute | solution.py:95
  10.2 10.4 %collective-permute-start = (bf16[96,1024]{1,0:T(8,128)(2,1)}, bf16[96,1024]{1,0:T(8,128)(2,1)S(1)}, u32[]{:S(2)}, u32[]{:S(2)}) collective-permute-start(bf16[96,1024]{1,0:T(8,128)(2,1)} %get-tuple-element.35.gated), channel_id=1, source_target_pairs={{0,2},{1,5},{2,0},{3,7},{4,6},{5,1},{6,4},{7,3},{8,10},{9,13},{10,... | collective-permute-start | bytes 589832 | tf_op jit(solution)/shard_map/ppermute | solution.py:95
  13.0 1.9 %copy-start = (bf16[384,4096]{1,0:T(8,128)(2,1)S(1)}, bf16[384,4096]{1,0:T(8,128)(2,1)}, u32[]{:S(2)}) copy-start(bf16[384,4096]{1,0:T(8,128)(2,1)} %tokens.1) | copy-start | bytes 9437188
  14.9 0.9 %copy-start.1 = (bf16[96,1024]{1,0:T(8,128)(2,1)S(1)}, bf16[96,1024]{1,0:T(8,128)(2,1)}, u32[]{:S(2)}) copy-start(bf16[96,1024]{1,0:T(8,128)(2,1)} %get-tuple-element.35.gated) | copy-start | bytes 589828
  16.4 8.0 %collective-permute-start.5 = (bf16[112,1024]{1,0:T(8,128)(2,1)S(1)}, bf16[112,1024]{1,0:T(8,128)(2,1)S(1)}, u32[]{:S(2)}, u32[]{:S(2)}) collective-permute-start(bf16[112,1024]{1,0:T(8,128)(2,1)S(1)} %collective-permute-done.4.refs_0_), channel_id=1, source_target_pairs={{0,2},{1,5},{2,0},{3,7},{4,6},{5,1},{6,4},{7,3},{8,10},{9,13},{10,... | collective-permute-start | bytes 688136 | tf_op jit(solution)/shard_map/ppermute | solution.py:95
  19.1 6.0 %collective-permute-start.7 = (bf16[112,1024]{1,0:T(8,128)(2,1)S(1)}, bf16[112,1024]{1,0:T(8,128)(2,1)S(1)}, u32[]{:S(2)}, u32[]{:S(2)}) collective-permute-start(bf16[112,1024]{1,0:T(8,128)(2,1)S(1)} %collective-permute-done.4.refs_0_), channel_id=1, source_target_pairs={{0,4},{1,3},{2,6},{3,1},{4,0},{5,7},{6,2},{7,5},{8,12},{9,11},{10,... | collective-permute-start | bytes 688136 | tf_op jit(solution)/shard_map/ppermute | solution.py:95
  20.6 6.6 %collective-permute-start.2 = (bf16[96,1024]{1,0:T(8,128)(2,1)S(1)}, bf16[96,1024]{1,0:T(8,128)(2,1)S(1)}, u32[]{:S(2)}, u32[]{:S(2)}) collective-permute-start(bf16[96,1024]{1,0:T(8,128)(2,1)S(1)} %collective-permute-done.refs_1_), channel_id=1, source_target_pairs={{0,4},{1,3},{2,6},{3,1},{4,0},{5,7},{6,2},{7,5},{8,12},{9,11},{10,... | collective-permute-start | bytes 589832 | tf_op jit(solution)/shard_map/ppermute | solution.py:95
  21.1 8.5 %collective-permute-start.10 = (bf16[96,1024]{1,0:T(8,128)(2,1)S(1)}, bf16[96,1024]{1,0:T(8,128)(2,1)S(1)}, u32[]{:S(2)}, u32[]{:S(2)}) collective-permute-start(bf16[96,1024]{1,0:T(8,128)(2,1)S(1)} %collective-permute-done.6.refs_0_), channel_id=1, source_target_pairs={{0,24},{1,25},{2,26},{3,27},{4,28},{5,29},{6,30},{7,31},{8,0},{9,1... | collective-permute-start | bytes 589832 | tf_op jit(solution)/shard_map/ppermute | solution.py:95
  25.1 10.3 %collective-permute-start.8 = (bf16[112,1024]{1,0:T(8,128)(2,1)S(1)}, bf16[112,1024]{1,0:T(8,128)(2,1)S(1)}, u32[]{:S(2)}, u32[]{:S(2)}) collective-permute-start(bf16[112,1024]{1,0:T(8,128)(2,1)S(1)} %collective-permute-done.5.refs_1_), channel_id=1, source_target_pairs={{0,4},{1,3},{2,6},{3,1},{4,0},{5,7},{6,2},{7,5},{8,12},{9,11},{10,... | collective-permute-start | bytes 688136 | tf_op jit(solution)/shard_map/ppermute | solution.py:95
  27.2 6.0 %collective-permute-start.9 = (bf16[96,1024]{1,0:T(8,128)(2,1)S(1)}, bf16[96,1024]{1,0:T(8,128)(2,1)S(1)}, u32[]{:S(2)}, u32[]{:S(2)}) collective-permute-start(bf16[96,1024]{1,0:T(8,128)(2,1)S(1)} %collective-permute-done.6.refs_0_), channel_id=1, source_target_pairs={{0,2},{1,5},{2,0},{3,7},{4,6},{5,1},{6,4},{7,3},{8,10},{9,13},{10,... | collective-permute-start | bytes 589832 | tf_op jit(solution)/shard_map/ppermute | solution.py:95
  29.6 7.8 %collective-permute-start.13 = (bf16[96,1024]{1,0:T(8,128)(2,1)S(1)}, bf16[96,1024]{1,0:T(8,128)(2,1)S(1)}, u32[]{:S(2)}, u32[]{:S(2)}) collective-permute-start(bf16[96,1024]{1,0:T(8,128)(2,1)S(1)} %collective-permute-done.10.refs_0_), channel_id=1, source_target_pairs={{0,2},{1,5},{2,0},{3,7},{4,6},{5,1},{6,4},{7,3},{8,10},{9,13},{10,... | collective-permute-start | bytes 589832 | tf_op jit(solution)/shard_map/ppermute | solution.py:95
  30.6 9.1 %collective-permute-start.11 = (bf16[96,1024]{1,0:T(8,128)(2,1)S(1)}, bf16[96,1024]{1,0:T(8,128)(2,1)S(1)}, u32[]{:S(2)}, u32[]{:S(2)}) collective-permute-start(bf16[96,1024]{1,0:T(8,128)(2,1)S(1)} %collective-permute-done.6.refs_0_), channel_id=1, source_target_pairs={{0,4},{1,3},{2,6},{3,1},{4,0},{5,7},{6,2},{7,5},{8,12},{9,11},{10,... | collective-permute-start | bytes 589832 | tf_op jit(solution)/shard_map/ppermute | solution.py:95
  33.3 6.4 %collective-permute-start.12 = (bf16[96,1024]{1,0:T(8,128)(2,1)S(1)}, bf16[96,1024]{1,0:T(8,128)(2,1)S(1)}, u32[]{:S(2)}, u32[]{:S(2)}) collective-permute-start(bf16[96,1024]{1,0:T(8,128)(2,1)S(1)} %collective-permute-done.9.refs_1_), channel_id=1, source_target_pairs={{0,4},{1,3},{2,6},{3,1},{4,0},{5,7},{6,2},{7,5},{8,12},{9,11},{10,... | collective-permute-start | bytes 589832 | tf_op jit(solution)/shard_map/ppermute | solution.py:95
  35.5 6.2 %collective-permute-start.14 = (bf16[96,1024]{1,0:T(8,128)(2,1)S(1)}, bf16[96,1024]{1,0:T(8,128)(2,1)S(1)}, u32[]{:S(2)}, u32[]{:S(2)}) collective-permute-start(bf16[96,1024]{1,0:T(8,128)(2,1)S(1)} %collective-permute-done.10.refs_0_), channel_id=1, source_target_pairs={{0,4},{1,3},{2,6},{3,1},{4,0},{5,7},{6,2},{7,5},{8,12},{9,11},{10,... | collective-permute-start | bytes 589832 | tf_op jit(solution)/shard_map/ppermute | solution.py:95
  37.4 6.3 %collective-permute-start.19 = (bf16[96,1024]{1,0:T(8,128)(2,1)S(1)}, bf16[96,1024]{1,0:T(8,128)(2,1)S(1)}, u32[]{:S(2)}, u32[]{:S(2)}) collective-permute-start(bf16[96,1024]{1,0:T(8,128)(2,1)S(1)} %collective-permute-done.13.refs_1_), channel_id=1, source_target_pairs={{0,4},{1,3},{2,6},{3,1},{4,0},{5,7},{6,2},{7,5},{8,12},{9,11},{10,... | collective-permute-start | bytes 589832 | tf_op jit(solution)/shard_map/ppermute | solution.py:95
  39.7 4.1 %collective-permute-start.16 = (f32[208,384]{1,0:T(8,128)S(1)}, f32[208,384]{1,0:T(8,128)S(1)}, u32[]{:S(2)}, u32[]{:S(2)}) collective-permute-start(f32[208,384]{1,0:T(8,128)S(1)} %get-tuple-element.53), channel_id=1, source_target_pairs={{0,1},{1,0},{2,3},{3,2},{4,5},{5,4},{6,7},{7,6},{8,9},{9,8},{10,11... | collective-permute-start | bytes 958472 | tf_op jit(solution)/shard_map/ppermute | solution.py:95
  40.9 3.8 %collective-permute-start.17 = (f32[192,384]{1,0:T(8,128)S(1)}, f32[192,384]{1,0:T(8,128)S(1)}, u32[]{:S(2)}, u32[]{:S(2)}) collective-permute-start(f32[192,384]{1,0:T(8,128)S(1)} %get-tuple-element.54), channel_id=1, source_target_pairs={{0,1},{1,0},{2,3},{3,2},{4,5},{5,4},{6,7},{7,6},{8,9},{9,8},{10,11... | collective-permute-start | bytes 884744 | tf_op jit(solution)/shard_map/ppermute | solution.py:95
  41.5 3.2 %collective-permute-start.15 = (f32[192,384]{1,0:T(8,128)S(1)}, f32[192,384]{1,0:T(8,128)S(1)}, u32[]{:S(2)}, u32[]{:S(2)}) collective-permute-start(f32[192,384]{1,0:T(8,128)S(1)} %get-tuple-element.52), channel_id=1, source_target_pairs={{0,1},{1,0},{2,3},{3,2},{4,5},{5,4},{6,7},{7,6},{8,9},{9,8},{10,11... | collective-permute-start | bytes 884744 | tf_op jit(solution)/shard_map/ppermute | solution.py:95
  42.9 1.8 %collective-permute-start.18 = (f32[192,384]{1,0:T(8,128)S(1)}, f32[192,384]{1,0:T(8,128)S(1)}, u32[]{:S(2)}, u32[]{:S(2)}) collective-permute-start(f32[192,384]{1,0:T(8,128)S(1)} %get-tuple-element.55), channel_id=1, source_target_pairs={{0,1},{1,0},{2,3},{3,2},{4,5},{5,4},{6,7},{7,6},{8,9},{9,8},{10,11... | collective-permute-start | bytes 884744 | tf_op jit(solution)/shard_map/ppermute | solution.py:95
  43.8 1.4 %collective-permute-start.20 = (bf16[96,1024]{1,0:T(8,128)(2,1)S(1)}, bf16[96,1024]{1,0:T(8,128)(2,1)S(1)}, u32[]{:S(2)}, u32[]{:S(2)}) collective-permute-start(bf16[96,1024]{1,0:T(8,128)(2,1)S(1)} %collective-permute-done.19.refs_8_), channel_id=1, source_target_pairs={{0,1},{1,0},{2,3},{3,2},{4,5},{5,4},{6,7},{7,6},{8,9},{9,8},{10,11... | collective-permute-start | bytes 589832 | tf_op jit(solution)/shard_map/ppermute | solution.py:95
